TPU v7x, 32 devices: a whole 2x2x4 slice. The times are simulated.
32 devices in a mesh: groups: 2 (over y), expert: 8 (over z, x), hidden: 2 (over core).
Axes of the slice: x: 2, y: 2, z: 4, core: 2. Of those that a mesh axis runs over, the one named last changes fastest.
Arguments:
- current: bfloat16 [2048, 2048], P(('groups', 'expert'), 'hidden'), parts along dimension 0, may hold values from -6 to 6
- previous: float32 [2048, 2048], P(('groups', 'expert'), 'hidden'), parts along dimension 0, may hold values from -6 to 6
- expert_ids: int32 [2048, 8], P(('groups', 'expert')), parts along dimension 0, may hold values from 0 to 15, all different within a row; in each aligned block of 128 rows (0 to 127, 128 to 255, ...) at most 72 rows name the same one
- gate_values: float32 [2048, 8], P(('groups', 'expert')), parts along dimension 0, may hold values from 0.1 to 1
- norm_gain: float32 [2048], replicated, may hold values from 0.1 to 1.9
- expert_gate: bfloat16 [16, 2048, 768], P('expert', 'hidden'), may hold values from -0.125 to 0.125
- expert_up: bfloat16 [16, 2048, 768], P('expert', 'hidden'), may hold values from -0.125 to 0.125
- expert_down: bfloat16 [16, 768, 2048], P('expert', None, 'hidden'), may hold values from -0.21875 to 0.21875
- dense_gate: bfloat16 [2048, 3072], P('expert', 'hidden'), may hold values from -0.125 to 0.125
- dense_up: bfloat16 [2048, 3072], P('expert', 'hidden'), may hold values from -0.125 to 0.125
- dense_down: bfloat16 [3072, 2048], P('hidden', 'expert'), may hold values from -0.109375 to 0.109375
Outputs:
- layer_out: bfloat16 [2048, 2048], P(('groups', 'expert'), 'hidden'), parts along dimension 0
There are 2 independent parts, one for each index of `groups`. A program takes and returns all parts, laid end to end along the dimension named above; an argument that names none is the same for every part. Nothing has to cross between parts.
Inputs may be any that keep to these rules, and one draw needn't show every extreme that they name: `expert_ids`: each row names 8 different experts. Within the rows of one index of the expert axis (aligned blocks of 128 rows) no expert is named by more than 72 rows, and in every draw some expert is named by exactly 72 rows of some block.
All inputs are finite; a program needn't handle non-finite values.
Results may differ from a plain program's by a relative error of at most 0.02.
Values may be sent and summed in bfloat16 or wider, within the bound.
A program may use at most 64 MiB of HBM per device.

v0:
```python
import jax
import jax.numpy as jnp
from jax import lax
from jax.sharding import PartitionSpec as P

TOP_K = 8


def slot_places(expert_ids, experts_all, owned, owners, capacity):
    flat_ids = expert_ids.reshape(-1)
    one_hot = (flat_ids[:, None] == jnp.arange(experts_all, dtype=jnp.int32)[None, :]).astype(
        jnp.int32
    )
    before = jnp.cumsum(one_hot, axis=0) - one_hot
    position = jnp.sum(before * one_hot, axis=1)
    return flat_ids % owned * (owners * capacity) + flat_ids // owned * capacity + position


def routed_branch(previous, expert_ids, gate_values, expert_gate, expert_up, expert_down):
    tokens_here, slice_width = previous.shape
    owned = expert_gate.shape[0]
    owners = lax.axis_size("expert")
    experts_all = owned * owners
    capacity = min(tokens_here, tokens_here * TOP_K * 9 // (8 * experts_all))
    places = slot_places(expert_ids, experts_all, owned, owners, capacity)
    token_of = jnp.arange(tokens_here * TOP_K, dtype=jnp.int32) // TOP_K
    table = jnp.full((experts_all * capacity,), tokens_here, jnp.int32).at[places].set(token_of)
    routed = previous.astype(jnp.bfloat16)
    routed_pad = jnp.concatenate([routed, jnp.zeros((1, slice_width), jnp.bfloat16)], axis=0)
    outgoing = routed_pad[table].reshape(owned, owners, capacity, slice_width)
    arrived = lax.all_to_all(outgoing, "expert", split_axis=1, concat_axis=1, tiled=True)
    arrived = arrived.reshape(owned, owners * capacity, slice_width)
    gate_part = jnp.einsum("erd,edf->erf", arrived, expert_gate, preferred_element_type=jnp.float32)
    up_part = jnp.einsum("erd,edf->erf", arrived, expert_up, preferred_element_type=jnp.float32)
    gate_sum, up_sum = (
        lax.psum(gate_part.astype(jnp.bfloat16), "hidden").astype(jnp.float32),
        lax.psum(up_part.astype(jnp.bfloat16), "hidden").astype(jnp.float32),
    )
    activated = (jax.nn.silu(gate_sum) * up_sum).astype(jnp.bfloat16)
    produced = jnp.einsum(
        "erf,efd->erd", activated, expert_down, preferred_element_type=jnp.float32
    ).astype(jnp.bfloat16)
    produced = produced.reshape(owned, owners, capacity, slice_width)
    returned = lax.all_to_all(produced, "expert", split_axis=1, concat_axis=1, tiled=True)
    returned = returned.reshape(experts_all * capacity, slice_width)
    picked = returned[places].reshape(tokens_here, TOP_K, slice_width).astype(jnp.float32)
    return jnp.einsum("tk,tkd->td", gate_values, picked)


def dense_branch(current, norm_gain, dense_gate, dense_up, dense_down):
    whole = lax.all_gather(current, "hidden", axis=1, tiled=True)
    wide = whole.astype(jnp.float32)
    mean_square = jnp.mean(wide * wide, axis=1, keepdims=True)
    normed = (wide * norm_gain[None, :] / jnp.sqrt(mean_square + 1e-06)).astype(jnp.bfloat16)
    full_gate, full_up = (
        lax.all_gather(dense_gate, "expert", axis=0, tiled=True),
        lax.all_gather(dense_up, "expert", axis=0, tiled=True),
    )
    gate_dense = jnp.dot(normed, full_gate, preferred_element_type=jnp.float32)
    up_dense = jnp.dot(normed, full_up, preferred_element_type=jnp.float32)
    dense_act = (jax.nn.silu(gate_dense) * up_dense).astype(jnp.bfloat16)
    terms = jnp.dot(
        dense_act,
        lax.all_gather(dense_down, "expert", axis=1, tiled=True),
        preferred_element_type=jnp.float32,
    )
    return lax.psum_scatter(
        terms.astype(jnp.bfloat16), "hidden", scatter_dimension=1, tiled=True
    ).astype(jnp.float32)


def local(
    current,
    previous,
    expert_ids,
    gate_values,
    norm_gain,
    expert_gate,
    expert_up,
    expert_down,
    dense_gate,
    dense_up,
    dense_down,
):
    routed_sum = routed_branch(
        previous, expert_ids, gate_values, expert_gate, expert_up, expert_down
    )
    dense_sum = dense_branch(current, norm_gain, dense_gate, dense_up, dense_down)
    return (dense_sum + routed_sum).astype(jnp.bfloat16)


def solution(mesh):
    placed = (
        P(("groups", "expert"), "hidden"),
        P(("groups", "expert"), "hidden"),
        P(("groups", "expert"), None),
        P(("groups", "expert"), None),
        P(),
        P("expert", "hidden", None),
        P("expert", "hidden", None),
        P("expert", None, "hidden"),
        P("expert", "hidden"),
        P("expert", "hidden"),
        P("hidden", "expert"),
    )
    return jax.shard_map(
        local,
        mesh=mesh,
        in_specs=placed,
        out_specs=P(("groups", "expert"), "hidden"),
        check_vma=False,
    )
```

profile of v0, /device:TPU:0, one launch (start us, length us, event | category | flops | bytes accessed | tf_op | source)
XLA Modules:
  0.0 468.2 jit_solution(6606188487306504337)
XLA Ops:
  7.4 0.0 copy-start
  7.4 0.0 all-reduce.4.cloned.1.call-start
  7.4 0.9 copy.19
  8.3 0.1 eq.31
  8.4 0.1 eq.27
  8.5 0.1 reshape.164
  8.6 4.5 reduce-window.6
  13.1 0.1 slice.12
  13.2 0.1 copy.22
  13.4 0.1 copy.23
  13.5 0.1 broadcast_add_fusion
  13.6 4.3 scatter_custom_fusion
  18.0 1.1 convert_element_type.52
  19.1 5.0 %gather_fusion = bf16[1152,1024]{1,0:T(8,128)(2,1)} fusion(bf16[129,1024]{1,0:T(8,128)(2,1)S(1)} %concatenate.3, s32[2048]{0:T(1024)S(1)} %pad_clamp_fusion), kind=kCustom, calls=%fused_computation | custom fusion | bytes 4723200 | tf_op jit(solution)/shard_map/gather | solution.py:30
  24.1 1.9 copy.24
  26.0 60.9 %all_to_all.10 = bf16[2,8,72,1024]{3,2,0,1:T(8,128)(2,1)S(1)} all-to-all(bf16[2,8,72,1024]{3,2,0,1:T(8,128)(2,1)S(1)} %copy.24), channel_id=1, replica_groups=mesh['groups'=2,'expert'=8,'hidden'=2] {'expert'}, dimensions={1} | all-to-all | bytes 4718592 | tf_op jit(solution)/shard_map/all_to_all | solution.py:31
  86.9 0.3 copy.25
  87.2 1.6 copy-done.4
  88.8 3.2 convolution_convert_fusion.2
  92.0 3.3 convolution_convert_fusion.3
  95.3 0.0 all-reduce.4.cloned.1.call-update
  95.3 0.0 all-gather.4.cloned.1.call-start
  95.4 0.5 all-gather.4.cloned.1.call-update
  95.9 0.0 all-gather.6.cloned.1.call-start
  96.0 0.5 all-gather.6.cloned.1.call-update
  96.5 0.0 all-gather.8.cloned.1.call-start
  96.5 0.5 all-gather.8.cloned.1.call-update
  97.1 21.5 %all-reduce.4.cloned.1.call-done = (bf16[2,576,768]{2,1,0:T(8,128)(2,1)}, bf16[2,576,768]{2,1,0:T(8,128)(2,1)}) async-done(((bf16[2,576,768]{2,1,0:T(8,128)(2,1)}, bf16[2,576,768]{2,1,0:T(8,128)(2,1)}), (bf16[2,576,768]{2,1,0:T(8,128)(2,1)}, bf16[2,576,768]{2,1,0:T(8,128)(2,1)})) %all-reduce.4.cloned.1.call-update) | async-done | bytes 3538960 | tf_op jit(solution)/shard_map/psum | solution.py:37
  118.5 4.3 convolution_convert_fusion.1
  122.8 1.7 copy.26
  124.5 5.9 %all-to-all-start.1 = ((bf16[2,8,72,1024]{3,2,0,1:T(8,128)(2,1)}), bf16[2,8,72,1024]{3,2,0,1:T(8,128)(2,1)}, u32[]{:S(2)}, u32[]{:S(2)}) async-start(bf16[2,8,72,1024]{3,2,0,1:T(8,128)(2,1)} %copy.26), calls=%async_computation.2 | async-start | bytes 4718592 | tf_op jit(solution)/shard_map/all_to_all | solution.py:44
  130.4 0.0 reduce-scatter.2.cloned.1.call-start
  130.5 2.4 all_gather.12
  132.9 0.8 copy-done.1
  133.6 0.2 fusion.12
  133.8 103.1 %all-gather.4.cloned.1.call-done = bf16[2048,1536]{1,0:T(8,128)(2,1)} async-done(((bf16[256,1536]{1,0:T(8,128)(2,1)}), bf16[2048,1536]{1,0:T(8,128)(2,1)}) %all-gather.4.cloned.1.call-update) | async-done | bytes 6291472 | tf_op jit(solution)/shard_map/all_gather | solution.py:56
  236.9 0.0 copy-done.6
  236.9 4.9 %fusion.31 = f32[128,1536]{1,0:T(8,128)} fusion(bf16[2048,1536]{1,0:T(8,128)(2,1)} %all-gather.4.cloned.1.call-done, bf16[128,2048]{1,0:T(8,128)(2,1)} %copy-done.1, f32[128]{0:T(128)S(1)} %add_sqrt_fusion, f32[2048]{0:T(1024)S(1)} %copy-done.6), kind=kOutput, calls=%fused_computation.59 | convolution fusion | flops 806354944 | bytes 7610880 | tf_op jit(solution)/shard_map/dot_general | solution.py:59
  241.8 94.5 %all-gather.6.cloned.1.call-done = bf16[2048,1536]{1,0:T(8,128)(2,1)} async-done(((bf16[256,1536]{1,0:T(8,128)(2,1)}), bf16[2048,1536]{1,0:T(8,128)(2,1)}) %all-gather.6.cloned.1.call-update) | async-done | bytes 6291472 | tf_op jit(solution)/shard_map/all_gather | solution.py:57
  336.4 99.8 %all-gather.8.cloned.1.call-done = bf16[1536,2048]{1,0:T(8,128)(2,1)} async-done(((bf16[1536,256]{1,0:T(8,128)(2,1)}), bf16[1536,2048]{1,0:T(8,128)(2,1)}) %all-gather.8.cloned.1.call-update) | async-done | bytes 6291472 | tf_op jit(solution)/shard_map/all_gather | solution.py:64
  436.2 7.8 %convolution_convert_fusion = bf16[128,2048]{1,0:T(8,128)(2,1)} fusion(bf16[1536,2048]{1,0:T(8,128)(2,1)} %all-gather.8.cloned.1.call-done, bf16[2048,1536]{1,0:T(8,128)(2,1)} %all-gather.6.cloned.1.call-done, f32[128,1536]{1,0:T(8,128)} %fusion.31, bf16[128,2048]{1,0:T(8,128)(2,1)} %copy-done.1, f32[128]{0:T(128)S(1)} %add_sqrt_fusion, f32[2048]{0:T(1024)S(1)} %copy-done.6), kind=kOutput, calls=%fused_computation.12 | convolution fusion | flops 1613103104 | bytes 14426624 | tf_op jit(solution)/shard_map/dot_general | solution.py:62
  444.0 0.0 reduce-scatter.2.cloned.1.call-update
  444.0 0.1 copy.28
  444.2 0.0 all-to-all-done.1
  444.2 3.3 copy.27
  447.5 8.1 %gather_fusion.1 = bf16[1024,1024]{1,0:T(8,128)(2,1)} fusion(bf16[1152,1024]{1,0:T(8,128)(2,1)} %bitcast.41, s32[1024]{0:T(1024)S(1)} %broadcast_clamp_fusion), kind=kCustom, calls=%fused_computation.1 | custom fusion | bytes 4198400 | tf_op jit(solution)/shard_map/gather | solution.py:46
  455.6 3.1 fusion.6
  458.7 1.9 fusion.13
  (22 shorter events, 0.2 us)
Async XLA Ops:
  7.4 111.2 %copy-start = (bf16[2,768,1024]{2,1,0:T(8,128)(2,1)S(1)}, bf16[2,768,1024]{2,1,0:T(8,128)(2,1)}, u32[]{:S(2)}) copy-start(bf16[2,768,1024]{2,1,0:T(8,128)(2,1)} %param.18) | copy-start | bytes 9437188
  7.4 111.2 %all-reduce.4.cloned.1.call-start = ((), (), s32[]{:S(2)}) async-start(), calls=%async_computation.7 | async-start | bytes 7077888 | tf_op jit(solution)/shard_map/psum | solution.py:37
  86.9 1.9 copy-start.4
  88.8 3.2 copy-start.5
  95.3 141.6 %all-gather.4.cloned.1.call-start = ((), (), s32[]{:S(2)}) async-start(), calls=%async_computation.3 | async-start | bytes 7077888 | tf_op jit(solution)/shard_map/all_gather | solution.py:56
  95.9 240.4 %all-gather.6.cloned.1.call-start = ((), (), s32[]{:S(2)}) async-start(), calls=%async_computation.4 | async-start | bytes 7077888 | tf_op jit(solution)/shard_map/all_gather | solution.py:57
  96.5 339.7 %all-gather.8.cloned.1.call-start = ((), (), s32[]{:S(2)}) async-start(), calls=%async_computation.5 | async-start | bytes 7077888 | tf_op jit(solution)/shard_map/all_gather | solution.py:64
  124.5 6.0 %copy-start.2 = (bf16[128,1024]{1,0:T(8,128)(2,1)S(1)}, bf16[128,1024]{1,0:T(8,128)(2,1)}, u32[]{:S(2)}) copy-start(bf16[128,1024]{1,0:T(8,128)(2,1)} %param.11) | copy-start | bytes 786436
  124.5 112.4 %copy-start.6 = (f32[2048]{0:T(1024)S(1)}, f32[2048]{0:T(1024)}, u32[]{:S(2)}) copy-start(f32[2048]{0:T(1024)} %param.15) | copy-start | bytes 24580
  124.5 319.7 %all-to-all-start.1 = ((bf16[2,8,72,1024]{3,2,0,1:T(8,128)(2,1)}), bf16[2,8,72,1024]{3,2,0,1:T(8,128)(2,1)}, u32[]{:S(2)}, u32[]{:S(2)}) async-start(bf16[2,8,72,1024]{3,2,0,1:T(8,128)(2,1)} %copy.26), calls=%async_computation.2 | async-start | bytes 4718592 | tf_op jit(solution)/shard_map/all_to_all | solution.py:44
  130.4 328.2 %reduce-scatter.2.cloned.1.call-start = ((), (), s32[]{:S(2)}) async-start(), calls=%async_computation.6 | async-start | bytes 786432 | tf_op jit(solution)/shard_map/reduce_scatter | solution.py:67
  132.9 0.8 copy-start.1
  241.8 202.2 %copy-start.3 = (f32[128,8]{0,1:T(8,128)S(1)}, f32[128,8]{0,1:T(8,128)}, u32[]{:S(2)}) copy-start(f32[128,8]{0,1:T(8,128)} %param.14) | copy-start | bytes 12292
Sparse Core Ops, SparseCore 0:
  95.5 23.0 all-reduce.3
  444.1 6.1 reduce-scatter.1
Sparse Core Ops, SparseCore 1:
  98.2 138.6 all-gather.3
  239.2 97.1 all-gather.5
  338.5 97.7 all-gather.7
where the time goes:
time: 469 us; the launch traced here: 468 us
  waiting for transfers between devices  321 us (68%)
  blocking collectives  63.3 us (13%)
  local copies, waits for them, and re-layouts  28.7 us (6%)
  matrix products  26.5 us (6%)
  between operations  15.2 us (3%)
  other arithmetic  7.93 us (2%)
  starting transfers between devices  6.07 us (1%)
    all_gather x1, waiting for transfers between devices, dense_branch(): lax.all_gather(dense_gate, 'expert', axis=0, tiled=True)  103 us
    all_gather x1, waiting for transfers between devices, dense_branch(): lax.all_gather(dense_down, 'expert', axis=1, tiled=True)  99.8 us
    all_gather x1, waiting for transfers between devices, dense_branch(): lax.all_gather(dense_up, 'expert', axis=0, tiled=True)  94.5 us
    all_to_all x1, blocking collectives, routed_branch(): lax.all_to_all(outgoing, 'expert', split_axis=1, concat_axis=1, tiled=True)  60.9 us
    psum x1, waiting for transfers between devices, routed_branch(): lax.psum(up_part.astype(jnp.bfloat16), 'hidden').astype(jnp.float32)  21.5 us
  transfers between devices with their start and end apart: 6, of which 4 were waited for; matrix products, arithmetic and copies ran while one was open for 7% of the time, Pallas kernels for 0%

commit v1 on v0

v1 whole, which is shorter than its diff:
```python
import jax
import jax.numpy as jnp
from jax import lax
from jax.sharding import PartitionSpec as P


def own_gates(expert_ids, gate_values, experts_all):
    hit = expert_ids[:, :, None] == jnp.arange(experts_all, dtype=jnp.int32)[None, None, :]
    return jnp.sum(jnp.where(hit, gate_values[:, :, None], 0.0), axis=1)


def normalize(current, norm_gain):
    width = current.shape[1]
    wide = current.astype(jnp.float32)
    total = lax.psum(jnp.sum(wide * wide, axis=1, keepdims=True), "hidden")
    mean_square = total / norm_gain.shape[0]
    gain = lax.dynamic_slice_in_dim(norm_gain, lax.axis_index("hidden") * width, width)
    return (wide * gain[None, :] / jnp.sqrt(mean_square + 1e-06)).astype(jnp.bfloat16)


def swiglu(rows, gate, up):
    gate_sum = jnp.dot(rows, gate, preferred_element_type=jnp.float32)
    up_sum = jnp.dot(rows, up, preferred_element_type=jnp.float32)
    return jax.nn.silu(gate_sum) * up_sum


def local(
    current,
    previous,
    expert_ids,
    gate_values,
    norm_gain,
    expert_gate,
    expert_up,
    expert_down,
    dense_gate,
    dense_up,
    dense_down,
):
    owned = expert_gate.shape[0]
    owners = lax.axis_size("expert")
    bf16 = jnp.bfloat16
    routed = previous.astype(bf16)
    normed = normalize(current, norm_gain)
    gates = own_gates(expert_ids, gate_values, owned * owners)
    swap = lambda w, axis, cut, join: lax.all_to_all(w, axis, split_axis=cut, concat_axis=join, tiled=True)
    wg = swap(expert_gate, "hidden", 2, 1)
    wu = swap(expert_up, "hidden", 2, 1)
    wd = swap(expert_down, "hidden", 1, 2)
    both = lax.all_gather(jnp.stack([routed, normed]), "expert", axis=1, tiled=True)
    both = lax.all_gather(both, "hidden", axis=2, tiled=True)
    mine = swap(gates, "expert", 1, 0)
    dg = swap(dense_gate, "expert", 1, 0)
    du = swap(dense_up, "expert", 1, 0)
    dd = swap(dense_down, "expert", 0, 1)
    acts = [
        (swiglu(both[0], wg[j], wu[j]) * mine[:, j : j + 1]).astype(bf16) for j in range(owned)
    ]
    acts.append(swiglu(both[1], dg, du).astype(bf16))
    downs = [wd[j] for j in range(owned)] + [dd]
    total = jnp.dot(
        jnp.concatenate(acts, axis=1), jnp.concatenate(downs, axis=0), preferred_element_type=jnp.float32
    ).astype(bf16)
    half = lax.psum_scatter(total, "hidden", scatter_dimension=1, tiled=True)
    return lax.psum_scatter(half, "expert", scatter_dimension=0, tiled=True)


def solution(mesh):
    placed = (
        P(("groups", "expert"), "hidden"),
        P(("groups", "expert"), "hidden"),
        P(("groups", "expert"), None),
        P(("groups", "expert"), None),
        P(),
        P("expert", "hidden", None),
        P("expert", "hidden", None),
        P("expert", None, "hidden"),
        P("expert", "hidden"),
        P("expert", "hidden"),
        P("hidden", "expert"),
    )
    return jax.shard_map(
        local,
        mesh=mesh,
        in_specs=placed,
        out_specs=P(("groups", "expert"), "hidden"),
        check_vma=False,
    )
```

time: 469 us -> 343 us (0.73)
  waiting for transfers between devices: 321 us -> 184 us
  local copies, waits for them, and re-layouts: 28.7 us -> 59.8 us
  blocking collectives: 63.3 us -> 43.4 us
  starting transfers between devices: 6.07 us -> 16.1 us
  matrix products: 26.5 us -> 19.6 us
    all_gather x3 -> x2, waiting for transfers between devices: 297 us -> 76.1 us  [the longest x1 76.1 us: local(): lax.all_gather(jnp.stack([routed, normed]), 'expert', axis=1, tiled=True)]
    reduce_scatter x1 -> x2, waiting for transfers between devices: 0.01 us -> 86.7 us  [the longest x1 73.3 us: local(): return lax.psum_scatter(half, 'expert', scatter_dimension=0, tiled=True)]
    unnamed x16 -> x33, local copies, waits for them, and re-layouts: 3.51 us -> 30.9 us
    all_to_all x1 -> x4, waiting for transfers between devices: 0.01 us -> 21.5 us  [local(): lax.all_to_all(w, axis, split_axis=cut, concat_axis=join, tiled=True)]
    psum x1 -> x0, waiting for transfers between devices: 21.5 us -> none  [routed_branch(): lax.psum(up_part.astype(jnp.bfloat16), 'hidden').astype(jnp.float32)]
    all_to_all x1 -> x3, blocking collectives: 60.9 us -> 40.8 us  [local(): lax.all_to_all(w, axis, split_axis=cut, concat_axis=join, tiled=True)]
    slice x2 -> x10, local copies, waits for them, and re-layouts: 0.21 us -> 17.8 us  [the longest x3 7.19 us: local(): wu[j]]
    gather x2 -> x0, local copies, waits for them, and re-layouts: 13.1 us -> none  [the longest x1 8.08 us: routed_branch(): returned[places].reshape(tokens_here, TOP_K, slice_width)]
  transfers between devices with their start and end apart: 6 -> 8, of which waited for: 4 -> 5; matrix products, arithmetic and copies ran while one was open for 7% -> 16% of each run, Pallas kernels for 0% -> 0%
where the time goes in v1:
time: 343 us; the launch traced here: 341 us
  waiting for transfers between devices  184 us (54%)
  local copies, waits for them, and re-layouts  59.8 us (17%)
  blocking collectives  43.4 us (13%)
  matrix products  19.6 us (6%)
  starting transfers between devices  16.1 us (5%)
  between operations  13.4 us (4%)
  other arithmetic  4.68 us (1%)
    all_gather x1, waiting for transfers between devices, local(): lax.all_gather(jnp.stack([routed, normed]), 'expert', axis=1, tiled=True)  76.1 us
    reduce_scatter x1, waiting for transfers between devices, local(): return lax.psum_scatter(half, 'expert', scatter_dimension=0, tiled=True)  73.3 us
    all_to_all x3, blocking collectives, local(): lax.all_to_all(w, axis, split_axis=cut, concat_axis=join, tiled=True)  40.8 us
    unnamed x33, local copies, waits for them, and re-layouts  30.9 us
    all_to_all x4, waiting for transfers between devices, local(): lax.all_to_all(w, axis, split_axis=cut, concat_axis=join, tiled=True)  21.5 us
    all_to_all x4, starting transfers between devices, local(): lax.all_to_all(w, axis, split_axis=cut, concat_axis=join, tiled=True)  16 us
    reduce_scatter x1, waiting for transfers between devices, local(): half = lax.psum_scatter(total, 'hidden', scatter_dimension=1, tiled=True)  13.4 us
    all_to_all x6, local copies, waits for them, and re-layouts, local(): lax.all_to_all(w, axis, split_axis=cut, concat_axis=join, tiled=True)  10.4 us
  transfers between devices with their start and end apart: 8, of which 5 were waited for; matrix products, arithmetic and copies ran while one was open for 16% of the time, Pallas kernels for 0%

profile of v1, /device:TPU:0, one launch (start us, length us, event | category | flops | bytes accessed | tf_op | source)
XLA Modules:
  0.0 341.4 jit_solution(6318909956214219701)
XLA Ops:
  6.5 1.1 fusion.24
  7.6 2.6 psum.7
  10.2 1.1 convert_bitcast_fusion
  11.3 0.7 dynamic_slice.3
  12.0 1.1 fusion.25
  13.0 0.8 pad_maximum_fusion
  14.0 76.1 %all-gather.3.cloned.1.call-done = bf16[2,1024,1024]{2,1,0:T(8,128)(2,1)} async-done(((bf16[2,128,1024]{2,1,0:T(8,128)(2,1)}), bf16[2,1024,1024]{2,1,0:T(8,128)(2,1)}) %all-gather.3.cloned.1.call-update) | async-done | bytes 4194320 | tf_op jit(solution)/shard_map/all_gather | solution.py:50
  90.1 1.9 copy-done.2
  91.9 6.0 %copy.58 = bf16[2,1024,768]{1,0,2:T(2,128)(2,1)} copy(bf16[2,1024,768]{2,1,0:T(8,128)(2,1)S(1)} %copy-done.2) | data formatting | bytes 6291456 | tf_op args[5]
  98.0 4.3 %all-to-all-start = ((bf16[2,1024,768]{1,0,2:T(2,128)(2,1)}), bf16[2,1024,768]{1,0,2:T(2,128)(2,1)S(1)}, u32[]{:S(2)}, u32[]{:S(2)}) async-start(bf16[2,1024,768]{1,0,2:T(2,128)(2,1)} %copy.58), calls=%async_computation | async-start | bytes 6291456 | tf_op jit(solution)/shard_map/all_to_all | solution.py:46
  102.2 9.0 %copy.61 = bf16[2,1024,768]{1,0,2:T(2,128)(2,1)} copy(bf16[2,1024,768]{2,1,0:T(8,128)(2,1)} %param.17) | data formatting | bytes 6291456 | tf_op args[6]
  111.2 6.8 %copy.70 = bf16[2,768,1024]{2,0,1:T(2,128)(2,1)} copy(bf16[2,768,1024]{2,1,0:T(8,128)(2,1)} %param.18) | data formatting | bytes 6291456 | tf_op args[7]
  118.1 0.6 select_reduce_fusion
  118.7 1.6 copy-done
  120.3 10.6 %all_to_all.121 = bf16[2,1024,768]{1,0,2:T(2,128)(2,1)} all-to-all(bf16[2,1024,768]{1,0,2:T(2,128)(2,1)} %copy.61), channel_id=1, replica_groups=mesh['groups'=2,'expert'=8,'hidden'=2] {'hidden'}, dimensions={2} | all-to-all | bytes 6291456 | tf_op jit(solution)/shard_map/all_to_all | solution.py:46
  130.9 6.2 %all_to_all.122 = bf16[2,768,1024]{2,0,1:T(2,128)(2,1)S(1)} all-to-all(bf16[2,768,1024]{2,0,1:T(2,128)(2,1)S(1)} %copy-done.1), channel_id=1, replica_groups=mesh['groups'=2,'expert'=8,'hidden'=2] {'hidden'}, dimensions={1} | all-to-all | bytes 6291456 | tf_op jit(solution)/shard_map/all_to_all | solution.py:46
  137.2 3.3 all-to-all-start.2
  140.5 2.3 copy.66
  142.8 4.2 %all-to-all-done.2 = f32[128,8,2]{0,2,1:T(2,128)S(1)} async-done(((f32[128,8,2]{0,2,1:T(2,128)}), f32[128,8,2]{0,2,1:T(2,128)S(1)}, u32[]{:S(2)}, u32[]{:S(2)}) %all-to-all-start.2) | async-done | bytes 8224 | tf_op jit(solution)/shard_map/all_to_all | solution.py:46
  147.0 4.2 %all-to-all-start.3 = ((bf16[256,8,192]{0,2,1:T(8,128)(2,1)}), bf16[256,8,192]{0,2,1:T(8,128)(2,1)}, u32[]{:S(2)}, u32[]{:S(2)}) async-start(bf16[256,8,192]{0,2,1:T(8,128)(2,1)} %bitcast.67), calls=%async_computation.3 | async-start | bytes 1572864 | tf_op jit(solution)/shard_map/all_to_all | solution.py:46
  151.2 2.3 copy.68
  153.5 17.4 %all-to-all-done.3 = bf16[256,8,192]{0,2,1:T(8,128)(2,1)} async-done(((bf16[256,8,192]{0,2,1:T(8,128)(2,1)}), bf16[256,8,192]{0,2,1:T(8,128)(2,1)}, u32[]{:S(2)}, u32[]{:S(2)}) %all-to-all-start.3) | async-done | bytes 786464 | tf_op jit(solution)/shard_map/all_to_all | solution.py:46
  170.9 23.9 %all_to_all.123 = bf16[256,8,192]{0,2,1:T(8,128)(2,1)} all-to-all(bf16[256,8,192]{0,2,1:T(8,128)(2,1)} %bitcast.68), channel_id=1, replica_groups=mesh['groups'=2,'expert'=8,'hidden'=2] {'expert'}, dimensions={1} | all-to-all | bytes 1572864 | tf_op jit(solution)/shard_map/all_to_all | solution.py:46
  194.8 4.2 %all-to-all-start.6 = ((bf16[8,192,256]{2,1,0:T(8,128)(2,1)}), bf16[8,192,256]{2,1,0:T(8,128)(2,1)}, u32[]{:S(2)}, u32[]{:S(2)}) async-start(bf16[8,192,256]{2,1,0:T(8,128)(2,1)} %bitcast.76), calls=%async_computation.6 | async-start | bytes 1572864 | tf_op jit(solution)/shard_map/all_to_all | solution.py:46
  199.1 2.8 copy.59
  201.9 1.9 fusion.28
  203.9 2.6 copy.64
  206.4 2.8 copy.62
  209.3 2.0 fusion.27
  211.3 2.6 copy.65
  213.9 2.6 copy.60
  216.5 2.6 copy.63
  219.1 1.0 copy.71
  220.4 1.6 copy.72
  221.9 1.6 copy.73
  223.5 1.2 copy.78
  224.7 1.0 copy.79
  225.7 1.6 copy.76
  227.4 4.2 %fusion.12 = f32[1024,384]{0,1:T(8,128)S(1)} fusion(bf16[2048,384]{1,0:T(8,128)(2,1)S(1)} %bitcast.71, bf16[2,1024,2048]{2,1,0:T(8,128)(2,1)} %all-gather.5.cloned.1.call-done), kind=kOutput, calls=%fused_computation.12 | convolution fusion | flops 1610612736 | bytes 7340032 | tf_op jit(solution)/shard_map/dot_general | solution.py:22
  231.6 0.9 copy-done.13
  232.5 1.9 fusion.14
  234.4 1.6 fusion.10
  236.0 1.6 fusion.21
  237.6 2.1 multiply_convert_fusion
  239.7 2.1 multiply_convert_fusion.1
  241.8 6.2 %fusion.6 = bf16[1024,2048]{1,0:T(8,128)(2,1)} fusion(bf16[192,2048]{0,1:T(8,128)(2,1)S(1)} %bitcast.75, bf16[384,2048]{0,1:T(8,128)(2,1)S(1)} %bitcast.73, bf16[384,2048]{0,1:T(8,128)(2,1)S(1)} %bitcast.72, bf16[1024,192]{0,1:T(8,128)(2,1)S(1)} %fusion.21, bf16[1024,384]{0,1:T(8,128)(2,1)S(1)} %multiply_convert_fusion, ...), kind=kOutput, calls=%fused_computation.8 | convolution fusion | flops 4046323712 | bytes 10092544 | tf_op jit(solution)/shard_map/dot_general | solution.py:61
  248.1 13.4 %reduce-scatter.3.cloned.1.call-done = bf16[1024,1024]{1,0:T(8,128)(2,1)} async-done(((bf16[1024,2048]{1,0:T(8,128)(2,1)}), bf16[1024,1024]{1,0:T(8,128)(2,1)}) %reduce-scatter.3.cloned.1.call-update) | async-done | bytes 2097168 | tf_op jit(solution)/shard_map/reduce_scatter | solution.py:64
  261.5 73.3 %reduce-scatter.5.cloned.1.call-done = bf16[128,1024]{1,0:T(8,128)(2,1)} async-done(((bf16[1024,1024]{1,0:T(8,128)(2,1)}), bf16[128,1024]{1,0:T(8,128)(2,1)}) %reduce-scatter.5.cloned.1.call-update) | async-done | bytes 262160 | tf_op jit(solution)/shard_map/reduce_scatter | solution.py:65
  (39 shorter events, 0.6 us)
Async XLA Ops:
  6.5 83.5 %all-gather.3.cloned.1.call-start = ((), (), s32[]{:S(2)}) async-start(), calls=%async_computation.9 | async-start | bytes 4718592 | tf_op jit(solution)/shard_map/all_gather | solution.py:50
  13.9 213.5 %all-gather.5.cloned.1.call-start = ((), (), s32[]{:S(2)}) async-start(), calls=%async_computation.10 | async-start | bytes 12582912 | tf_op jit(solution)/shard_map/all_gather | solution.py:51
  90.0 1.9 copy-start.2
  98.0 20.7 %all-to-all-start = ((bf16[2,1024,768]{1,0,2:T(2,128)(2,1)}), bf16[2,1024,768]{1,0,2:T(2,128)(2,1)S(1)}, u32[]{:S(2)}, u32[]{:S(2)}) async-start(bf16[2,1024,768]{1,0,2:T(2,128)(2,1)} %copy.58), calls=%async_computation | async-start | bytes 6291456 | tf_op jit(solution)/shard_map/all_to_all | solution.py:46
  111.2 6.9 %copy-start.11 = (f32[128,8]{0,1:T(8,128)S(1)}, f32[128,8]{0,1:T(8,128)}, u32[]{:S(2)}) copy-start(f32[128,8]{0,1:T(8,128)} %param.14) | copy-start | bytes 12292
  111.2 6.9 %copy-start.12 = (s32[128,8]{0,1:T(8,128)S(1)}, s32[128,8]{0,1:T(8,128)}, u32[]{:S(2)}) copy-start(s32[128,8]{0,1:T(8,128)} %param.13) | copy-start | bytes 12292
  118.7 1.6 copy-start
  120.3 10.6 %copy-start.1 = (bf16[2,768,1024]{2,0,1:T(2,128)(2,1)S(1)}, bf16[2,768,1024]{2,0,1:T(2,128)(2,1)}, u32[]{:S(2)}) copy-start(bf16[2,768,1024]{2,0,1:T(2,128)(2,1)} %copy.70) | copy-start | bytes 9437188
  137.2 9.8 %all-to-all-start.2 = ((f32[128,8,2]{0,2,1:T(2,128)}), f32[128,8,2]{0,2,1:T(2,128)S(1)}, u32[]{:S(2)}, u32[]{:S(2)}) async-start(f32[128,8,2]{0,2,1:T(2,128)} %bitcast.11), calls=%async_computation.2 | async-start | bytes 16384 | tf_op jit(solution)/shard_map/all_to_all | solution.py:46
  147.0 23.9 %all-to-all-start.3 = ((bf16[256,8,192]{0,2,1:T(8,128)(2,1)}), bf16[256,8,192]{0,2,1:T(8,128)(2,1)}, u32[]{:S(2)}, u32[]{:S(2)}) async-start(bf16[256,8,192]{0,2,1:T(8,128)(2,1)} %bitcast.67), calls=%async_computation.3 | async-start | bytes 1572864 | tf_op jit(solution)/shard_map/all_to_all | solution.py:46
  194.8 30.9 %all-to-all-start.6 = ((bf16[8,192,256]{2,1,0:T(8,128)(2,1)}), bf16[8,192,256]{2,1,0:T(8,128)(2,1)}, u32[]{:S(2)}, u32[]{:S(2)}) async-start(bf16[8,192,256]{2,1,0:T(8,128)(2,1)} %bitcast.76), calls=%async_computation.6 | async-start | bytes 1572864 | tf_op jit(solution)/shard_map/all_to_all | solution.py:46
  199.0 62.5 %reduce-scatter.3.cloned.1.call-start = ((), (), s32[]{:S(2)}) async-start(), calls=%async_computation.11 | async-start | bytes 6291456 | tf_op jit(solution)/shard_map/reduce_scatter | solution.py:64
  221.9 2.8 copy-start.3
  224.7 2.7 copy-start.6
  227.4 4.2 %copy-start.9 = (bf16[1,2,1024,384]{3,2,1,0:T(8,128)(2,1)S(1)}, bf16[1,2,1024,384]{3,2,1,0:T(8,128)(2,1)}, u32[]{:S(2)}) copy-start(bf16[1,2,1024,384]{3,2,1,0:T(8,128)(2,1)} %copy.60) | copy-start | bytes 4718596
  227.4 5.1 %copy-start.13 = (bf16[2,1024,2048]{2,1,0:T(8,128)(2,1)S(1)}, bf16[2,1024,2048]{2,1,0:T(8,128)(2,1)}, u32[]{:S(2)}) copy-start(bf16[2,1024,2048]{2,1,0:T(8,128)(2,1)} %all-gather.5.cloned.1.call-done) | copy-start | bytes 25165828
  234.4 1.6 copy-start.10
  236.0 1.6 copy-start.4
  237.6 2.1 copy-start.5
  239.7 2.1 copy-start.7
  239.7 2.1 copy-start.8
  248.1 86.8 %reduce-scatter.5.cloned.1.call-start = ((), (), s32[]{:S(2)}) async-start(), calls=%async_computation.12 | async-start | bytes 2359296 | tf_op jit(solution)/shard_map/reduce_scatter | solution.py:65
Sparse Core Ops, SparseCore 0:
  14.0 75.9 all-gather.2
  91.6 19.4 all-gather.4
  248.2 13.2 reduce-scatter.2
  265.3 69.4 reduce-scatter.4

commit v2 on v1

--- a/solution.py
+++ b/solution.py
@@ -1,7 +1,341 @@
+import functools
+
 import jax
 import jax.numpy as jnp
 from jax import lax
+from jax.experimental import pallas as pl
+from jax.experimental.pallas import tpu as pltpu
 from jax.sharding import PartitionSpec as P
+
+MESH = pl.DeviceIdType.MESH
+
+
+def ring_place(index, n):
+    odd = lax.rem(index, 2)
+    level = lax.div(index, 2)
+    return (1 - odd) * level + odd * (n - 1 - level)
+
+
+def ring_index(place, n):
+    place = lax.rem(place + 2 * n, n)
+    back = lax.div(place, n // 2)
+    return (1 - back) * 2 * place + back * (2 * (n - 1 - place) + 1)
+
+
+def rows_of(index, size):
+    return pl.ds(pl.multiple_of(index * size, size), size)
+
+
+def greet(peers):
+    barrier = pltpu.get_barrier_semaphore()
+    for peer in peers:
+        pl.semaphore_signal(barrier, inc=1, device_id=peer, device_id_type=MESH)
+    pl.semaphore_wait(barrier, len(peers))
+
+
+def remote(src, dst, send, recv, peer):
+    return pltpu.make_async_remote_copy(
+        src_ref=src, dst_ref=dst, send_sem=send, recv_sem=recv, device_id=peer, device_id_type=MESH
+    )
+
+
+def gather_kernel(
+    n, tok, gates, gu, dn, eg, eu, ed, all_tok, all_gates, w1, wd, w2,
+    ring_s, ring_r, core_s, core_r, exp_s, exp_r, push_s, push_r, fwd_s, fwd_r, here,
+):
+    me, h, g = lax.axis_index("expert"), lax.axis_index("hidden"), lax.axis_index("groups")
+    kinds, tokens, width = tok.shape
+    owned, _, hidden_units = eg.shape
+    share = hidden_units // 2
+    depth, units = gu.shape[1], dn.shape[1]
+    half = n // 2
+    place = ring_place(me, n)
+    right, left = {"expert": ring_index(place + 1, n)}, {"expert": ring_index(place - 1, n)}
+    mate, twin = {"hidden": 1 - h}, {"groups": 1 - g}
+    greet([{"expert": lax.rem(me + d, n)} for d in range(1, n)] + [mate, twin])
+    pending = []
+    mine = pl.ds(pl.multiple_of(h * width, width), width)
+
+    def start(copy):
+        copy.start()
+        pending.append(copy)
+
+    def block(t, origin, lo, size):
+        rows = pl.ds(pl.multiple_of(origin * tokens + lo, size), size)
+        return all_tok.at[t, rows, mine]
+
+    def span(step, way):
+        if step < half:
+            return 0, tokens
+        return way * (tokens // 2), tokens // 2
+
+    def hop(t, step, way):
+        origin = ring_index(place - (step - 1) if way == 0 else place + (step - 1), n)
+        lo, size = span(step, way)
+        src = tok.at[t, pl.ds(lo, size)] if step == 1 else block(t, origin, lo, size)
+        k = (t * 2 + way) * half + step - 1
+        return remote(src, block(t, origin, lo, size), ring_s.at[k], ring_r.at[k], right if way == 0 else left)
+
+    def to_mate(t, origin, lo, size, k, src=None):
+        view = block(t, origin, lo, size)
+        k = t * (n + 1) + k
+        start(remote(view if src is None else src, view, core_s.at[k], core_r.at[k], mate))
+
+    for t in range(kinds):
+        for way in range(2):
+            start(hop(t, 1, way))
+    locals_ = []
+
+    def keep(src, dst):
+        copy = pltpu.make_async_copy(src, dst, here.at[len(locals_)])
+        copy.start()
+        locals_.append(copy)
+
+    pushes = []
+    for d in range(1, n):
+        to = lax.rem(me + d, n)
+        peer = {"expert": to}
+        rows = pl.ds(pl.multiple_of(g * (depth // 2), depth // 2), depth // 2)
+        into = pl.ds(pl.multiple_of(me * depth + g * (depth // 2), depth // 2), depth // 2)
+        a = remote(gu.at[to, rows], wd.at[into], push_s.at[3 * d], push_r.at[3 * d], peer)
+        rows = pl.ds(pl.multiple_of(g * (units // 2), units // 2), units // 2)
+        into = pl.ds(pl.multiple_of(owned * share + g * (units // 2), 16), units // 2)
+        b = remote(
+            dn.at[to, rows], w2.at[into, rows_of(me, depth)], push_s.at[3 * d + 1], push_r.at[3 * d + 1], peer
+        )
+        c = remote(gates.at[to], all_gates.at[me], push_s.at[3 * d + 2], push_r.at[3 * d + 2], peer)
+        for copy in (a, b, c):
+            copy.start()
+        pushes.append((a, b, c))
+    swaps = []
+    for j in range(owned):
+        away = pl.ds(pl.multiple_of((1 - h) * share, 128), share)
+        stay = pl.ds(pl.multiple_of(h * share, 128), share)
+        for i, w in enumerate((eg, eu)):
+            spot = w1.at[rows_of(h, width), pl.ds((2 * j + i) * share, share)]
+            k = 3 * j + i
+            swaps.append(remote(w.at[j, :, away], spot, exp_s.at[k], exp_r.at[k], mate))
+            keep(w.at[j, :, stay], spot)
+        spot = w2.at[pl.ds(j * share, share), mine]
+        away = pl.ds(pl.multiple_of((1 - h) * share, 16), share)
+        stay = pl.ds(pl.multiple_of(h * share, 16), share)
+        swaps.append(remote(ed.at[j, away], spot, exp_s.at[3 * j + 2], exp_r.at[3 * j + 2], mate))
+        keep(ed.at[j, stay], spot)
+    for copy in swaps:
+        copy.start()
+    for t in range(kinds):
+        to_mate(t, me, 0, tokens, 0, tok.at[t])
+        keep(tok.at[t], block(t, me, 0, tokens))
+    keep(gu.at[me], wd.at[rows_of(me, depth)])
+    keep(dn.at[me], w2.at[pl.ds(owned * share, units), rows_of(me, depth)])
+    keep(gates.at[me], all_gates.at[me])
+
+    forwards = []
+
+    def pass_on(d):
+        for copy in pushes[d - 1]:
+            copy.wait_recv()
+        source = lax.rem(me - d + n, n)
+        into = pl.ds(pl.multiple_of(source * depth + g * (depth // 2), depth // 2), depth // 2)
+        a = remote(wd.at[into], wd.at[into], fwd_s.at[2 * d], fwd_r.at[2 * d], twin)
+        into = pl.ds(pl.multiple_of(owned * share + g * (units // 2), 16), units // 2)
+        spot = w2.at[into, rows_of(source, depth)]
+        b = remote(spot, spot, fwd_s.at[2 * d + 1], fwd_r.at[2 * d + 1], twin)
+        for copy in (a, b):
+            copy.start()
+            forwards.append(copy)
+
+    late = list(range(1, n))
+    for step in range(1, half + 1):
+        for t in range(kinds):
+            for way in range(2):
+                hop(t, step, way).wait_recv()
+                origin = ring_index(place - step if way == 0 else place + step, n)
+                lo, size = span(step, way)
+                if step < half:
+                    start(hop(t, step + 1, way))
+                to_mate(t, origin, lo, size, 2 * step - 1 + way)
+        if step > 1 and step < half:
+            for _ in range(2):
+                pass_on(late.pop(0))
+    while late:
+        pass_on(late.pop(0))
+    for copy in pending:
+        copy.wait_send()
+    for t in range(kinds):
+        for k in range(n + 1):
+            step, way = (k + 1) // 2, (k + 1) % 2
+            lo, size = (0, tokens) if k == 0 else span(step, way)
+            origin = ring_index(place if k == 0 else (place - step if way == 0 else place + step), n)
+            theirs = pl.ds(pl.multiple_of((1 - h) * width, width), width)
+            rows = pl.ds(pl.multiple_of(origin * tokens + lo, size), size)
+            view = all_tok.at[t, rows, theirs]
+            remote(view, view, core_s.at[t * (n + 1) + k], core_r.at[t * (n + 1) + k], mate).wait_recv()
+    for copy in swaps + forwards:
+        copy.wait()
+    for group in pushes:
+        for copy in group:
+            copy.wait_send()
+    for copy in locals_:
+        copy.wait()
+
+
+def gather(n, tok, gates, gu, dn, eg, eu, ed):
+    kinds, tokens, width = tok.shape
+    owned, _, hidden_units = eg.shape
+    depth, units = gu.shape[1], dn.shape[1]
+    share = hidden_units // 2
+    dma = lambda count: pltpu.SemaphoreType.DMA((count,))
+    shape = jax.ShapeDtypeStruct
+    bf16 = jnp.bfloat16
+    return pl.pallas_call(
+        functools.partial(gather_kernel, n),
+        out_shape=(
+            shape((kinds, n * tokens, 2 * width), bf16),
+            shape(gates.shape, gates.dtype),
+            shape((2 * width, 2 * owned * share), bf16),
+            shape((n * depth, gu.shape[2]), bf16),
+            shape((owned * share + units, 2 * width), bf16),
+        ),
+        in_specs=[pl.BlockSpec(memory_space=pl.ANY)] * 7,
+        out_specs=[pl.BlockSpec(memory_space=pl.ANY)] * 5,
+        scratch_shapes=[dma(kinds * n)] * 2
+        + [dma(kinds * (n + 1))] * 2
+        + [dma(3 * owned)] * 2
+        + [dma(3 * n)] * 2
+        + [dma(2 * n)] * 2
+        + [dma(3 * owned + kinds + 3)],
+        compiler_params=pltpu.CompilerParams(collective_id=0, has_side_effects=True),
+    )(tok, gates, gu, dn, eg, eu, ed)
+
+
+def reduce_kernel(n, part, out, core, sent, got, core_s, core_r, ring_s, ring_r):
+    me, h = lax.axis_index("expert"), lax.axis_index("hidden")
+    tokens, width = out.shape
+    half = n // 2
+    place = ring_place(me, n)
+    right, left = {"expert": ring_index(place + 1, n)}, {"expert": ring_index(place - 1, n)}
+    mate = {"hidden": 1 - h}
+    greet([right, left, mate])
+    mine = pl.ds(pl.multiple_of(h * width, width), width)
+    theirs = pl.ds(pl.multiple_of((1 - h) * width, width), width)
+    order = [half]
+    for d in range(half - 1, 0, -1):
+        order += [d, -d]
+    order.append(0)
+    trades = {}
+    for k, d in enumerate(order):
+        rows = rows_of(ring_index(place + d, n), tokens)
+        trades[d] = remote(part.at[rows, theirs], core.at[rows], core_s.at[k], core_r.at[k], mate)
+        trades[d].start()
+
+    def own(d):
+        trades[d].wait_recv()
+        rows = rows_of(ring_index(place + d, n), tokens)
+        return part[rows, mine].astype(jnp.float32) + core[rows].astype(jnp.float32)
+
+    def view(buffer, step, way):
+        k = way * half + step - 1
+        if step == 1:
+            return buffer.at[k, pl.ds(way * (tokens // 2), tokens // 2)]
+        return buffer.at[k]
+
+    def hop(step, way):
+        k = way * half + step - 1
+        return remote(
+            view(sent, step, way), view(got, step, way), ring_s.at[k], ring_r.at[k], right if way == 0 else left
+        )
+
+    far = own(half).astype(jnp.bfloat16)
+    hops = []
+    for step in range(1, half + 1):
+        for way in range(2):
+            k = way * half + step - 1
+            if step == 1:
+                lo = way * (tokens // 2)
+                sent[k, pl.ds(lo, tokens // 2)] = far[lo : lo + tokens // 2]
+            else:
+                d = half + 1 - step
+                value = own(d if way == 0 else -d)
+                hop(step - 1, way).wait_recv()
+                if step == 2:
+                    lo = way * (tokens // 2)
+                    other = tokens // 2 - lo
+                    cut = slice(lo, lo + tokens // 2)
+                    add = got[k - 1, pl.ds(lo, tokens // 2)].astype(jnp.float32)
+                    sent[k, pl.ds(lo, tokens // 2)] = (value[cut] + add).astype(jnp.bfloat16)
+                    sent[k, pl.ds(other, tokens // 2)] = value[other : other + tokens // 2].astype(jnp.bfloat16)
+                else:
+                    sent[k] = (value + got[k - 1].astype(jnp.float32)).astype(jnp.bfloat16)
+            copy = hop(step, way)
+            copy.start()
+            hops.append(copy)
+    value = own(0)
+    for way in range(2):
+        hop(half, way).wait_recv()
+        value = value + got[way * half + half - 1].astype(jnp.float32)
+    out[...] = value.astype(jnp.bfloat16)
+    for copy in hops:
+        copy.wait_send()
+    for copy in trades.values():
+        copy.wait_send()
+
+
+def reduce_sum(n, part):
+    tokens, width = part.shape[0] // n, part.shape[1] // 2
+    bf16 = jnp.bfloat16
+    dma = lambda count: pltpu.SemaphoreType.DMA((count,))
+    return pl.pallas_call(
+        functools.partial(reduce_kernel, n),
+        out_shape=jax.ShapeDtypeStruct((tokens, width), bf16),
+        in_specs=[pl.BlockSpec(memory_space=pltpu.VMEM)],
+        out_specs=pl.BlockSpec(memory_space=pltpu.VMEM),
+        scratch_shapes=[
+            pltpu.VMEM((n * tokens, width), bf16),
+            pltpu.VMEM((n, tokens, width), bf16),
+            pltpu.VMEM((n, tokens, width), bf16),
+            dma(n), dma(n), dma(n), dma(n),
+        ],
+        compiler_params=pltpu.CompilerParams(
+            collective_id=1, has_side_effects=True, vmem_limit_bytes=40 * 2**20
+        ),
+    )(part)
+
+
+def kernel_fits(tokens, width, share, depth, units):
+    pairs = lax.axis_size("hidden") == 2 and lax.axis_size("groups") == 2
+    even = lax.axis_size("expert") % 2 == 0 and lax.axis_size("expert") >= 4
+    aligned = tokens % 128 == 0 and width % 128 == 0 and share % 128 == 0
+    return pairs and even and aligned and depth % 128 == 0 and units % 32 == 0
+
+
+def by_kernels(routed, normed, gates, expert_gate, expert_up, expert_down, dense_gate, dense_up, dense_down):
+    n = lax.axis_size("expert")
+    tokens = routed.shape[0]
+    owned, _, hidden_units = expert_gate.shape
+    share = hidden_units // 2
+    depth, spread = dense_gate.shape
+    units = spread // n
+    bf16 = jnp.bfloat16
+    cut = lambda w: w.reshape(depth, n, units).transpose(1, 0, 2)
+    gu = jnp.concatenate([cut(dense_gate), cut(dense_up)], axis=2)
+    dn = dense_down.reshape(n, units, depth)
+    pad = -owned % 8
+    packed = jnp.pad(gates.T.reshape(n, owned, tokens), ((0, 0), (0, pad), (0, 0)))
+    rows, got, w1, wd, w2 = gather(
+        n, jnp.stack([routed, normed]), packed, gu, dn, expert_gate, expert_up, expert_down
+    )
+    scale = got[:, :owned].transpose(0, 2, 1).reshape(n * tokens, owned)
+    sums = jnp.dot(rows[0], w1, preferred_element_type=jnp.float32)
+    dense = jnp.dot(rows[1], wd, preferred_element_type=jnp.float32)
+    acts = []
+    for j in range(owned):
+        gate = sums[:, 2 * j * share : (2 * j + 1) * share]
+        up = sums[:, (2 * j + 1) * share : (2 * j + 2) * share]
+        acts.append((jax.nn.silu(gate) * up * scale[:, j : j + 1]).astype(bf16))
+    acts.append((jax.nn.silu(dense[:, :units]) * dense[:, units:]).astype(bf16))
+    part = jnp.dot(jnp.concatenate(acts, axis=1), w2, preferred_element_type=jnp.float32)
+    return reduce_sum(n, part.astype(bf16))
 
 
 def own_gates(expert_ids, gate_values, experts_all):
@@ -43,6 +377,11 @@
     routed = previous.astype(bf16)
     normed = normalize(current, norm_gain)
     gates = own_gates(expert_ids, gate_values, owned * owners)
+    share, units = expert_gate.shape[2] // 2, dense_gate.shape[1] // owners
+    if kernel_fits(*routed.shape, share, dense_gate.shape[0], units):
+        return by_kernels(
+            routed, normed, gates, expert_gate, expert_up, expert_down, dense_gate, dense_up, dense_down
+        )
     swap = lambda w, axis, cut, join: lax.all_to_all(w, axis, split_axis=cut, concat_axis=join, tiled=True)
     wg = swap(expert_gate, "hidden", 2, 1)
     wu = swap(expert_up, "hidden", 2, 1)

time: 343 us -> 241 us (0.70)
  Pallas kernels: 0 us -> 205 us
  waiting for transfers between devices: 184 us -> 0 us
  local copies, waits for them, and re-layouts: 59.8 us -> 6.38 us
  blocking collectives: 43.4 us -> 2.58 us
  starting transfers between devices: 16.1 us -> 0 us
  between operations: 13.4 us -> 0.12 us
    pallas_call x0 -> x2, Pallas kernels: none -> 205 us  [the longest x1 176 us: gather(): pl.pallas_call(functools.partial(gather_kernel, n), out_shape=(shape((kin...]
    reduce_scatter x2 -> x0, waiting for transfers between devices: 86.7 us -> none  [the longest x1 73.3 us: local(): return lax.psum_scatter(half, 'expert', scatter_dimension=0, tiled=True)]
    all_gather x2 -> x0, waiting for transfers between devices: 76.1 us -> none  [the longest x1 76.1 us: local(): lax.all_gather(jnp.stack([routed, normed]), 'expert', axis=1, tiled=True)]
    all_to_all x3 -> x0, blocking collectives: 40.8 us -> none  [local(): lax.all_to_all(w, axis, split_axis=cut, concat_axis=join, tiled=True)]
    unnamed x33 -> x13, local copies, waits for them, and re-layouts: 30.9 us -> 3.28 us
    all_to_all x4 -> x0, waiting for transfers between devices: 21.5 us -> none  [local(): lax.all_to_all(w, axis, split_axis=cut, concat_axis=join, tiled=True)]
    slice x10 -> x1, local copies, waits for them, and re-layouts: 17.8 us -> 0.01 us  [by_kernels(): acts.append((jax.nn.silu(gate) * up * scale[:, j:j + 1]).astype(bf16))]
    all_to_all x4 -> x0, starting transfers between devices: 16 us -> none  [local(): lax.all_to_all(w, axis, split_axis=cut, concat_axis=join, tiled=True)]
  transfers between devices with their start and end apart: 8 -> 0, of which waited for: 5 -> 0; matrix products, arithmetic and copies ran while one was open for 16% -> 0% of each run, Pallas kernels for 0% -> 0%
where the time goes in v2:
time: 241 us
  Pallas kernels  205 us (85%)
  matrix products  18.6 us (8%)
  other arithmetic  7.44 us (3%)
  local copies, waits for them, and re-layouts  6.38 us (3%)
  blocking collectives  2.58 us (1%)
    pallas_call x1, Pallas kernels, gather(): pl.pallas_call(functools.partial(gather_kernel, n), out_shape=(shape((kin...  176 us
    pallas_call x1, Pallas kernels, reduce_sum(): pl.pallas_call(functools.partial(reduce_kernel, n), out_shape=jax.ShapeDt...  29 us
    dot_general x1, matrix products, by_kernels(): sums = jnp.dot(rows[0], w1, preferred_element_type=jnp.float32)  8.76 us
    dot_general x1, matrix products, by_kernels(): dense = jnp.dot(rows[1], wd, preferred_element_type=jnp.float32)  5.14 us

profile of v2, /device:TPU:0, one launch (start us, length us, event | category | flops | bytes accessed | tf_op | source)
XLA Modules:
  0.0 240.5 jit_solution(5800606467825922232)
XLA Ops:
  0.0 0.0 copy-start.1
  0.0 0.0 copy-start.2
  0.0 0.0 copy-start
  0.0 1.2 fusion.18
  1.2 2.6 %psum.7 = f32[128,1]{0,1:T(1,128)S(1)} all-reduce(f32[128,1]{0,1:T(1,128)S(1)} %bitcast.38), channel_id=1, replica_groups=mesh['groups'=2,'expert'=8,'hidden'=2] {'hidden'}, use_global_device_ids=true, to_apply=%region_1.0 | all-reduce | flops 128 | bytes 1024 | tf_op jit(solution)/shard_map/psum | solution.py:349
  3.8 0.7 dynamic_slice.3
  4.5 1.1 fusion.19
  5.5 1.1 convert_bitcast_fusion
  6.6 0.8 pad_maximum_fusion.1.tok
  7.4 0.0 copy-done.1
  7.4 0.0 copy-done.2
  7.5 0.6 pad.4.gates
  8.1 0.0 copy-done
  8.1 0.3 copy.26
  8.4 0.5 copy.27
  8.9 1.4 copy.24
  10.3 0.5 copy.25
  10.8 1.7 pad_maximum_fusion.gu
  12.5 176.4 %shard_map.109 = (bf16[2,1024,2048]{2,1,0:T(8,128)(2,1)}, f32[8,8,128]{2,1,0:T(8,128)}, bf16[2048,1536]{1,0:T(8,128)(2,1)}, bf16[2048,384]{1,0:T(8,128)(2,1)}, bf16[960,2048]{1,0:T(8,128)(2,1)}) custom-call(bf16[2,128,1024]{2,1,0:T(8,128)(2,1)} %pad_maximum_fusion.1.tok, f32[8,8,128]{2,1,0:T(8,128)} %pad.4.gates, bf16[8,256,384]{2,1,0:T(8,128)(2,1)} %pad_maximum_fusion.gu, ...), custom_call_target="tpu_custom_call" | custom-call | tf_op jit(solution)/shard_map/pallas_call | solution.py:191
  189.0 0.0 copy-start.3
  189.0 5.1 %fusion = f32[1024,384]{1,0:T(8,128)S(1)} fusion(bf16[2048,384]{1,0:T(8,128)(2,1)} %get-tuple-element.13, bf16[2,1024,2048]{2,1,0:T(8,128)(2,1)} %get-tuple-element.10), kind=kOutput, calls=%fused_computation | convolution fusion | flops 1610612736 | bytes 7340032 | tf_op jit(solution)/shard_map/dot_general | solution.py:330
  194.1 0.3 fusion.15
  194.5 0.0 copy-done.3
  194.5 8.8 %fusion.2 = f32[1024,1536]{1,0:T(8,128)S(1)} fusion(bf16[2048,1536]{1,0:T(8,128)(2,1)} %get-tuple-element.11, bf16[2,1024,2048]{2,1,0:T(8,128)(2,1)S(1)} %copy-done.3), kind=kOutput, calls=%fused_computation.2 | convolution fusion | flops 6442450944 | bytes 16777216 | tf_op jit(solution)/shard_map/dot_general | solution.py:329
  203.2 0.8 slice_bitcast_fusion
  204.0 0.0 copy-start.4
  204.0 1.2 fusion.14
  205.2 0.9 copy-done.4
  206.1 4.7 %convolution_convert_fusion.part = bf16[1024,2048]{1,0:T(8,128)(2,1)S(1)} fusion(bf16[960,2048]{1,0:T(8,128)(2,1)S(1)} %copy-done.4, bf16[1024,192]{1,0:T(8,128)(2,1)S(1)} %fusion.15, bf16[1024,384]{1,0:T(8,128)(2,1)S(1)} %get-tuple-element.16, bf16[1024,384]{1,0:T(8,128)(2,1)S(1)} %get-tuple-element.15), kind=kOutput, calls=%fused_computation.6 | convolution fusion | flops 4034527232 | bytes 10092544 | tf_op jit(solution)/shard_map/dot_general | solution.py:337
  210.9 29.0 %shard_map.110 = bf16[128,1024]{1,0:T(8,128)(2,1)S(1)} custom-call(bf16[1024,2048]{1,0:T(8,128)(2,1)S(1)} %convolution_convert_fusion.part), custom_call_target="tpu_custom_call" | custom-call | tf_op jit(solution)/shard_map/pallas_call | solution.py:288
  239.8 0.7 copy.32
  (3 shorter events, 0.0 us)
Async XLA Ops:
  0.0 7.4 %copy-start.1 = (f32[128,8]{0,1:T(8,128)S(1)}, f32[128,8]{0,1:T(8,128)}, u32[]{:S(2)}) copy-start(f32[128,8]{0,1:T(8,128)} %param.14) | copy-start | bytes 12292
  0.0 7.4 %copy-start.2 = (s32[128,8]{0,1:T(8,128)S(1)}, s32[128,8]{0,1:T(8,128)}, u32[]{:S(2)}) copy-start(s32[128,8]{0,1:T(8,128)} %param.13) | copy-start | bytes 12292
  0.0 8.1 %copy-start = (bf16[256,1536]{1,0:T(8,128)(2,1)S(1)}, bf16[256,1536]{1,0:T(8,128)(2,1)}, u32[]{:S(2)}) copy-start(bf16[256,1536]{1,0:T(8,128)(2,1)} %param.20) | copy-start | bytes 2359300
  189.0 5.5 %copy-start.3 = (bf16[2,1024,2048]{2,1,0:T(8,128)(2,1)S(1)}, bf16[2,1024,2048]{2,1,0:T(8,128)(2,1)}, u32[]{:S(2)}) copy-start(bf16[2,1024,2048]{2,1,0:T(8,128)(2,1)} %get-tuple-element.10) | copy-start | bytes 25165828
  204.0 2.1 copy-start.4

commit v3 on v2

--- a/solution.py
+++ b/solution.py
@@ -108,21 +108,23 @@
             copy.start()
         pushes.append((a, b, c))
     swaps = []
-    for j in range(owned):
+
+    def swap_expert(j):
         away = pl.ds(pl.multiple_of((1 - h) * share, 128), share)
         stay = pl.ds(pl.multiple_of(h * share, 128), share)
         for i, w in enumerate((eg, eu)):
             spot = w1.at[rows_of(h, width), pl.ds((2 * j + i) * share, share)]
             k = 3 * j + i
             swaps.append(remote(w.at[j, :, away], spot, exp_s.at[k], exp_r.at[k], mate))
+            swaps[-1].start()
             keep(w.at[j, :, stay], spot)
         spot = w2.at[pl.ds(j * share, share), mine]
         away = pl.ds(pl.multiple_of((1 - h) * share, 16), share)
         stay = pl.ds(pl.multiple_of(h * share, 16), share)
         swaps.append(remote(ed.at[j, away], spot, exp_s.at[3 * j + 2], exp_r.at[3 * j + 2], mate))
+        swaps[-1].start()
         keep(ed.at[j, stay], spot)
-    for copy in swaps:
-        copy.start()
+
     for t in range(kinds):
         to_mate(t, me, 0, tokens, 0, tok.at[t])
         keep(tok.at[t], block(t, me, 0, tokens))
@@ -155,8 +157,11 @@
                 if step < half:
                     start(hop(t, step + 1, way))
                 to_mate(t, origin, lo, size, 2 * step - 1 + way)
-        if step > 1 and step < half:
-            for _ in range(2):
+        for j in range(owned):
+            if min(j + 1, half - 1) == step:
+                swap_expert(j)
+        if step == half - 1:
+            for _ in range(half - 1):
                 pass_on(late.pop(0))
     while late:
         pass_on(late.pop(0))

time: 241 us -> 242 us (level)
  no operation moved by 1% of the time
where the time goes in v3:
time: 242 us
  Pallas kernels  206 us (85%)
  matrix products  18.6 us (8%)
  other arithmetic  7.44 us (3%)
  local copies, waits for them, and re-layouts  6.38 us (3%)
  blocking collectives  2.58 us (1%)
    pallas_call x1, Pallas kernels, gather(): pl.pallas_call(functools.partial(gather_kernel, n), out_shape=(shape((kin...  176 us
    pallas_call x1, Pallas kernels, reduce_sum(): pl.pallas_call(functools.partial(reduce_kernel, n), out_shape=jax.ShapeDt...  30.1 us
    dot_general x1, matrix products, by_kernels(): sums = jnp.dot(rows[0], w1, preferred_element_type=jnp.float32)  8.76 us
    dot_general x1, matrix products, by_kernels(): dense = jnp.dot(rows[1], wd, preferred_element_type=jnp.float32)  5.14 us

profile of v3, /device:TPU:0, one launch (start us, length us, event | category | flops | bytes accessed | tf_op | source)
XLA Modules:
  0.0 241.6 jit_solution(10179619228343409537)
XLA Ops:
  0.0 0.0 copy-start.1
  0.0 0.0 copy-start.2
  0.0 0.0 copy-start
  0.0 1.2 fusion.18
  1.2 2.6 %psum.7 = f32[128,1]{0,1:T(1,128)S(1)} all-reduce(f32[128,1]{0,1:T(1,128)S(1)} %bitcast.38), channel_id=1, replica_groups=mesh['groups'=2,'expert'=8,'hidden'=2] {'hidden'}, use_global_device_ids=true, to_apply=%region_1.0 | all-reduce | flops 128 | bytes 1024 | tf_op jit(solution)/shard_map/psum | solution.py:354
  3.8 0.7 dynamic_slice.3
  4.5 1.1 fusion.19
  5.5 1.1 convert_bitcast_fusion
  6.6 0.8 pad_maximum_fusion.1.tok
  7.4 0.0 copy-done.1
  7.4 0.0 copy-done.2
  7.5 0.6 pad.4.gates
  8.1 0.0 copy-done
  8.1 0.3 copy.26
  8.4 0.5 copy.27
  8.9 1.4 copy.24
  10.3 0.5 copy.25
  10.8 1.7 pad_maximum_fusion.gu
  12.5 176.4 %shard_map.109 = (bf16[2,1024,2048]{2,1,0:T(8,128)(2,1)}, f32[8,8,128]{2,1,0:T(8,128)}, bf16[2048,1536]{1,0:T(8,128)(2,1)}, bf16[2048,384]{1,0:T(8,128)(2,1)}, bf16[960,2048]{1,0:T(8,128)(2,1)}) custom-call(bf16[2,128,1024]{2,1,0:T(8,128)(2,1)} %pad_maximum_fusion.1.tok, f32[8,8,128]{2,1,0:T(8,128)} %pad.4.gates, bf16[8,256,384]{2,1,0:T(8,128)(2,1)} %pad_maximum_fusion.gu, ...), custom_call_target="tpu_custom_call" | custom-call | tf_op jit(solution)/shard_map/pallas_call | solution.py:196
  189.0 0.0 copy-start.3
  189.0 5.1 %fusion = f32[1024,384]{1,0:T(8,128)S(1)} fusion(bf16[2048,384]{1,0:T(8,128)(2,1)} %get-tuple-element.13, bf16[2,1024,2048]{2,1,0:T(8,128)(2,1)} %get-tuple-element.10), kind=kOutput, calls=%fused_computation | convolution fusion | flops 1610612736 | bytes 7340032 | tf_op jit(solution)/shard_map/dot_general | solution.py:335
  194.1 0.3 fusion.15
  194.5 0.0 copy-done.3
  194.5 8.8 %fusion.2 = f32[1024,1536]{1,0:T(8,128)S(1)} fusion(bf16[2048,1536]{1,0:T(8,128)(2,1)} %get-tuple-element.11, bf16[2,1024,2048]{2,1,0:T(8,128)(2,1)S(1)} %copy-done.3), kind=kOutput, calls=%fused_computation.2 | convolution fusion | flops 6442450944 | bytes 16777216 | tf_op jit(solution)/shard_map/dot_general | solution.py:334
  203.3 0.8 slice_bitcast_fusion
  204.0 0.0 copy-start.4
  204.0 1.2 fusion.14
  205.3 0.9 copy-done.4
  206.1 4.7 %convolution_convert_fusion.part = bf16[1024,2048]{1,0:T(8,128)(2,1)S(1)} fusion(bf16[960,2048]{1,0:T(8,128)(2,1)S(1)} %copy-done.4, bf16[1024,192]{1,0:T(8,128)(2,1)S(1)} %fusion.15, bf16[1024,384]{1,0:T(8,128)(2,1)S(1)} %get-tuple-element.16, bf16[1024,384]{1,0:T(8,128)(2,1)S(1)} %get-tuple-element.15), kind=kOutput, calls=%fused_computation.6 | convolution fusion | flops 4034527232 | bytes 10092544 | tf_op jit(solution)/shard_map/dot_general | solution.py:342
  210.9 30.1 %shard_map.110 = bf16[128,1024]{1,0:T(8,128)(2,1)S(1)} custom-call(bf16[1024,2048]{1,0:T(8,128)(2,1)S(1)} %convolution_convert_fusion.part), custom_call_target="tpu_custom_call" | custom-call | tf_op jit(solution)/shard_map/pallas_call | solution.py:293
  240.9 0.7 copy.32
  (3 shorter events, 0.0 us)
Async XLA Ops:
  0.0 7.4 %copy-start.1 = (f32[128,8]{0,1:T(8,128)S(1)}, f32[128,8]{0,1:T(8,128)}, u32[]{:S(2)}) copy-start(f32[128,8]{0,1:T(8,128)} %param.14) | copy-start | bytes 12292
  0.0 7.4 %copy-start.2 = (s32[128,8]{0,1:T(8,128)S(1)}, s32[128,8]{0,1:T(8,128)}, u32[]{:S(2)}) copy-start(s32[128,8]{0,1:T(8,128)} %param.13) | copy-start | bytes 12292
  0.0 8.1 %copy-start = (bf16[256,1536]{1,0:T(8,128)(2,1)S(1)}, bf16[256,1536]{1,0:T(8,128)(2,1)}, u32[]{:S(2)}) copy-start(bf16[256,1536]{1,0:T(8,128)(2,1)} %param.20) | copy-start | bytes 2359300
  189.0 5.5 %copy-start.3 = (bf16[2,1024,2048]{2,1,0:T(8,128)(2,1)S(1)}, bf16[2,1024,2048]{2,1,0:T(8,128)(2,1)}, u32[]{:S(2)}) copy-start(bf16[2,1024,2048]{2,1,0:T(8,128)(2,1)} %get-tuple-element.10) | copy-start | bytes 25165828
  204.0 2.1 copy-start.4

commit v4 on v3

--- a/solution.py
+++ b/solution.py
@@ -203,14 +203,16 @@
             shape((owned * share + units, 2 * width), bf16),
         ),
         in_specs=[pl.BlockSpec(memory_space=pl.ANY)] * 7,
-        out_specs=[pl.BlockSpec(memory_space=pl.ANY)] * 5,
+        out_specs=[pl.BlockSpec(memory_space=pltpu.VMEM)] * 5,
         scratch_shapes=[dma(kinds * n)] * 2
         + [dma(kinds * (n + 1))] * 2
         + [dma(3 * owned)] * 2
         + [dma(3 * n)] * 2
         + [dma(2 * n)] * 2
         + [dma(3 * owned + kinds + 3)],
-        compiler_params=pltpu.CompilerParams(collective_id=0, has_side_effects=True),
+        compiler_params=pltpu.CompilerParams(
+            collective_id=0, has_side_effects=True, vmem_limit_bytes=48 * 2**20
+        ),
     )(tok, gates, gu, dn, eg, eu, ed)
 
 

time: 242 us -> 159 us (0.66)
  Pallas kernels: 206 us -> 127 us
    pallas_call x1, Pallas kernels: 176 us -> 92.3 us  [gather(): pl.pallas_call(functools.partial(gather_kernel, n), out_shape=(shape((kin...]
    pallas_call x1, Pallas kernels: 30.1 us -> 34.7 us  [reduce_sum(): pl.pallas_call(functools.partial(reduce_kernel, n), out_shape=jax.ShapeDt...]
where the time goes in v4:
time: 159 us
  Pallas kernels  127 us (80%)
  matrix products  18.2 us (11%)
  local copies, waits for them, and re-layouts  5.57 us (4%)
  other arithmetic  5.49 us (3%)
  blocking collectives  2.58 us (2%)
    pallas_call x1, Pallas kernels, gather(): pl.pallas_call(functools.partial(gather_kernel, n), out_shape=(shape((kin...  92.3 us
    pallas_call x1, Pallas kernels, reduce_sum(): pl.pallas_call(functools.partial(reduce_kernel, n), out_shape=jax.ShapeDt...  34.7 us
    dot_general x1, matrix products, by_kernels(): sums = jnp.dot(rows[0], w1, preferred_element_type=jnp.float32)  8.76 us
    dot_general x1, matrix products, by_kernels(): jnp.dot(jnp.concatenate(acts, axis=1), w2, preferred_element_type=jnp.flo...  4.75 us
    dot_general x1, matrix products, by_kernels(): dense = jnp.dot(rows[1], wd, preferred_element_type=jnp.float32)  4.66 us
    unnamed x15, local copies, waits for them, and re-layouts  3.83 us

profile of v4, /device:TPU:0, one launch (start us, length us, event | category | flops | bytes accessed | tf_op | source)
XLA Modules:
  0.0 159.0 jit_solution(14299770982317185419)
XLA Ops:
  0.0 0.0 copy-start.2
  0.0 0.0 copy-start.3
  0.0 0.0 copy-start.1
  0.0 1.2 fusion.18
  1.2 2.6 %psum.7 = f32[128,1]{0,1:T(1,128)S(1)} all-reduce(f32[128,1]{0,1:T(1,128)S(1)} %bitcast.38), channel_id=1, replica_groups=mesh['groups'=2,'expert'=8,'hidden'=2] {'hidden'}, use_global_device_ids=true, to_apply=%region_1.0 | all-reduce | flops 128 | bytes 1024 | tf_op jit(solution)/shard_map/psum | solution.py:356
  3.8 0.7 dynamic_slice.3
  4.5 1.1 fusion.19
  5.5 1.1 convert_bitcast_fusion
  6.6 0.1 pad_maximum_fusion.1.tok
  6.6 0.0 copy-done.2
  6.7 0.0 copy-done.3
  6.7 0.0 copy-done.1
  6.7 0.3 copy.26
  7.0 0.5 copy.27
  7.5 1.4 copy.24
  8.9 0.5 copy.25
  9.4 0.0 copy-start
  9.4 0.6 pad_maximum_fusion.gu
  10.0 0.5 copy-done
  10.6 92.3 %shard_map.109 = (bf16[2,1024,2048]{2,1,0:T(8,128)(2,1)}, f32[8,8,128]{2,1,0:T(8,128)S(1)}, bf16[2048,1536]{1,0:T(8,128)(2,1)}, bf16[2048,384]{1,0:T(8,128)(2,1)S(1)}, bf16[960,2048]{1,0:T(8,128)(2,1)}) custom-call(bf16[2,128,1024]{2,1,0:T(8,128)(2,1)S(1)} %pad_maximum_fusion.1.tok, f32[8,8,128]{2,1,0:T(8,128)S(1)} %pad.4.gates, ...), custom_call_target="tpu_custom_call" | custom-call | tf_op jit(solution)/shard_map/pallas_call | solution.py:196
  102.9 0.0 copy-start.4
  102.9 4.7 %fusion = f32[1024,384]{1,0:T(8,128)S(1)} fusion(bf16[2048,384]{1,0:T(8,128)(2,1)S(1)} %get-tuple-element.13, bf16[2,1024,2048]{2,1,0:T(8,128)(2,1)} %get-tuple-element.10), kind=kOutput, calls=%fused_computation | convolution fusion | flops 1610612736 | bytes 7340032 | tf_op jit(solution)/shard_map/dot_general | solution.py:337
  107.6 0.3 fusion.15
  107.9 0.0 copy-done.4
  107.9 8.8 %fusion.2 = f32[1024,1536]{1,0:T(8,128)S(1)} fusion(bf16[2048,1536]{1,0:T(8,128)(2,1)} %get-tuple-element.11, bf16[2,1024,2048]{2,1,0:T(8,128)(2,1)S(1)} %copy-done.4), kind=kOutput, calls=%fused_computation.2 | convolution fusion | flops 6442450944 | bytes 16777216 | tf_op jit(solution)/shard_map/dot_general | solution.py:336
  116.7 0.0 copy-start.5
  116.7 1.2 fusion.14
  117.9 0.9 copy-done.5
  118.8 4.8 %convolution_convert_fusion.part = bf16[1024,2048]{1,0:T(8,128)(2,1)S(1)} fusion(bf16[960,2048]{1,0:T(8,128)(2,1)S(1)} %copy-done.5, bf16[1024,192]{1,0:T(8,128)(2,1)S(1)} %fusion.15, bf16[1024,384]{1,0:T(8,128)(2,1)S(1)} %get-tuple-element.16, bf16[1024,384]{1,0:T(8,128)(2,1)S(1)} %get-tuple-element.15), kind=kOutput, calls=%fused_computation.6 | convolution fusion | flops 4034527232 | bytes 10092544 | tf_op jit(solution)/shard_map/dot_general | solution.py:344
  123.6 34.7 %shard_map.110 = bf16[128,1024]{1,0:T(8,128)(2,1)S(1)} custom-call(bf16[1024,2048]{1,0:T(8,128)(2,1)S(1)} %convolution_convert_fusion.part), custom_call_target="tpu_custom_call" | custom-call | tf_op jit(solution)/shard_map/pallas_call | solution.py:295
  158.3 0.7 copy.32
  (5 shorter events, 0.0 us)
Async XLA Ops:
  0.0 6.7 %copy-start.2 = (f32[128,8]{0,1:T(8,128)S(1)}, f32[128,8]{0,1:T(8,128)}, u32[]{:S(2)}) copy-start(f32[128,8]{0,1:T(8,128)} %param.14) | copy-start | bytes 12292
  0.0 6.7 %copy-start.3 = (s32[128,8]{0,1:T(8,128)S(1)}, s32[128,8]{0,1:T(8,128)}, u32[]{:S(2)}) copy-start(s32[128,8]{0,1:T(8,128)} %param.13) | copy-start | bytes 12292
  0.0 6.7 %copy-start.1 = (bf16[256,1536]{1,0:T(8,128)(2,1)S(1)}, bf16[256,1536]{1,0:T(8,128)(2,1)}, u32[]{:S(2)}) copy-start(bf16[256,1536]{1,0:T(8,128)(2,1)} %param.20) | copy-start | bytes 2359300
  9.4 1.1 copy-start
  102.9 5.0 %copy-start.4 = (bf16[2,1024,2048]{2,1,0:T(8,128)(2,1)S(1)}, bf16[2,1024,2048]{2,1,0:T(8,128)(2,1)}, u32[]{:S(2)}) copy-start(bf16[2,1024,2048]{2,1,0:T(8,128)(2,1)} %get-tuple-element.10) | copy-start | bytes 25165828
  116.7 2.1 %copy-start.5 = (bf16[960,2048]{1,0:T(8,128)(2,1)S(1)}, bf16[960,2048]{1,0:T(8,128)(2,1)}, u32[]{:S(2)}) copy-start(bf16[960,2048]{1,0:T(8,128)(2,1)} %get-tuple-element.14) | copy-start | bytes 11796484

commit v5 on v4

--- a/solution.py
+++ b/solution.py
@@ -40,7 +40,7 @@
 
 
 def gather_kernel(
-    n, tok, gates, gu, dn, eg, eu, ed, all_tok, all_gates, w1, wd, w2,
+    n, tok, gates, gu, dn, eg, eu, ed, acts, w2, all_tok, all_gates, w1, wd,
     ring_s, ring_r, core_s, core_r, exp_s, exp_r, push_s, push_r, fwd_s, fwd_r, here,
 ):
     me, h, g = lax.axis_index("expert"), lax.axis_index("hidden"), lax.axis_index("groups")
@@ -91,7 +91,7 @@
         copy.start()
         locals_.append(copy)
 
-    pushes = []
+    pushes, gate_copies = [], []
     for d in range(1, n):
         to = lax.rem(me + d, n)
         peer = {"expert": to}
@@ -104,9 +104,10 @@
             dn.at[to, rows], w2.at[into, rows_of(me, depth)], push_s.at[3 * d + 1], push_r.at[3 * d + 1], peer
         )
         c = remote(gates.at[to], all_gates.at[me], push_s.at[3 * d + 2], push_r.at[3 * d + 2], peer)
-        for copy in (a, b, c):
+        for copy in (c, a, b):
             copy.start()
-        pushes.append((a, b, c))
+        pushes.append((a, b))
+        gate_copies.append(c)
     swaps = []
 
     def swap_expert(j):
@@ -132,7 +133,47 @@
     keep(dn.at[me], w2.at[pl.ds(owned * share, units), rows_of(me, depth)])
     keep(gates.at[me], all_gates.at[me])
 
+    for j in range(owned):
+        swap_expert(j)
     forwards = []
+
+    def from_mate(t, k):
+        step, way = (k + 1) // 2, (k + 1) % 2
+        lo, size = (0, tokens) if k == 0 else span(step, way)
+        origin = ring_index(place if k == 0 else (place - step if way == 0 else place + step), n)
+        theirs = pl.ds(pl.multiple_of((1 - h) * width, width), width)
+        rows = pl.ds(pl.multiple_of(origin * tokens + lo, size), size)
+        view = all_tok.at[t, rows, theirs]
+        k = t * (n + 1) + k
+        remote(view, view, core_s.at[k], core_r.at[k], mate).wait_recv()
+
+    def swish(gate, up):
+        return gate / (1.0 + jnp.exp(-gate)) * up
+
+    def experts(first, count):
+        def body(i, carry):
+            origin = ring_index(place + first + i, n)
+            rows = rows_of(origin, tokens)
+            sums = jnp.dot(all_tok[0, rows], w1[...], preferred_element_type=jnp.float32)
+            scale = all_gates[origin].T
+            for j in range(owned):
+                gate = sums[:, 2 * j * share : (2 * j + 1) * share]
+                up = sums[:, (2 * j + 1) * share : (2 * j + 2) * share]
+                value = swish(gate, up) * scale[:, j : j + 1]
+                acts[rows, j * share : (j + 1) * share] = value.astype(jnp.bfloat16)
+            return carry
+
+        lax.fori_loop(0, count, body, 0)
+
+    def dense():
+        def body(i, carry):
+            rows = rows_of(i, 2 * tokens)
+            sums = jnp.dot(all_tok[1, rows], wd[...], preferred_element_type=jnp.float32)
+            value = swish(sums[:, :units], sums[:, units:])
+            acts[rows, owned * share : owned * share + units] = value.astype(jnp.bfloat16)
+            return carry
+
+        lax.fori_loop(0, n // 2, body, 0)
 
     def pass_on(d):
         for copy in pushes[d - 1]:
@@ -157,32 +198,33 @@
                 if step < half:
                     start(hop(t, step + 1, way))
                 to_mate(t, origin, lo, size, 2 * step - 1 + way)
-        for j in range(owned):
-            if min(j + 1, half - 1) == step:
-                swap_expert(j)
         if step == half - 1:
             for _ in range(half - 1):
                 pass_on(late.pop(0))
+            for copy in swaps:
+                copy.wait()
+            for copy in locals_:
+                copy.wait()
+            for copy in gate_copies:
+                copy.wait()
+            for k in range(2 * half - 3):
+                from_mate(0, k)
+            experts(2 - half, 2 * half - 3)
     while late:
         pass_on(late.pop(0))
+    for k in range(2 * half - 3, n + 1):
+        from_mate(0, k)
+    experts(half - 1, 3)
+    for k in range(n + 1):
+        from_mate(1, k)
+    for copy in forwards:
+        copy.wait()
+    dense()
     for copy in pending:
         copy.wait_send()
-    for t in range(kinds):
-        for k in range(n + 1):
-            step, way = (k + 1) // 2, (k + 1) % 2
-            lo, size = (0, tokens) if k == 0 else span(step, way)
-            origin = ring_index(place if k == 0 else (place - step if way == 0 else place + step), n)
-            theirs = pl.ds(pl.multiple_of((1 - h) * width, width), width)
-            rows = pl.ds(pl.multiple_of(origin * tokens + lo, size), size)
-            view = all_tok.at[t, rows, theirs]
-            remote(view, view, core_s.at[t * (n + 1) + k], core_r.at[t * (n + 1) + k], mate).wait_recv()
-    for copy in swaps + forwards:
-        copy.wait()
     for group in pushes:
         for copy in group:
             copy.wait_send()
-    for copy in locals_:
-        copy.wait()
 
 
 def gather(n, tok, gates, gu, dn, eg, eu, ed):
@@ -196,15 +238,18 @@
     return pl.pallas_call(
         functools.partial(gather_kernel, n),
         out_shape=(
-            shape((kinds, n * tokens, 2 * width), bf16),
-            shape(gates.shape, gates.dtype),
-            shape((2 * width, 2 * owned * share), bf16),
-            shape((n * depth, gu.shape[2]), bf16),
+            shape((n * tokens, owned * share + units), bf16),
             shape((owned * share + units, 2 * width), bf16),
         ),
         in_specs=[pl.BlockSpec(memory_space=pl.ANY)] * 7,
-        out_specs=[pl.BlockSpec(memory_space=pltpu.VMEM)] * 5,
-        scratch_shapes=[dma(kinds * n)] * 2
+        out_specs=[pl.BlockSpec(memory_space=pltpu.VMEM)] * 2,
+        scratch_shapes=[
+            pltpu.VMEM((kinds, n * tokens, 2 * width), bf16),
+            pltpu.VMEM(gates.shape, gates.dtype),
+            pltpu.VMEM((2 * width, 2 * owned * share), bf16),
+            pltpu.VMEM((n * depth, gu.shape[2]), bf16),
+        ]
+        + [dma(kinds * n)] * 2
         + [dma(kinds * (n + 1))] * 2
         + [dma(3 * owned)] * 2
         + [dma(3 * n)] * 2
@@ -329,19 +374,10 @@
     dn = dense_down.reshape(n, units, depth)
     pad = -owned % 8
     packed = jnp.pad(gates.T.reshape(n, owned, tokens), ((0, 0), (0, pad), (0, 0)))
-    rows, got, w1, wd, w2 = gather(
+    acts, w2 = gather(
         n, jnp.stack([routed, normed]), packed, gu, dn, expert_gate, expert_up, expert_down
     )
-    scale = got[:, :owned].transpose(0, 2, 1).reshape(n * tokens, owned)
-    sums = jnp.dot(rows[0], w1, preferred_element_type=jnp.float32)
-    dense = jnp.dot(rows[1], wd, preferred_element_type=jnp.float32)
-    acts = []
-    for j in range(owned):
-        gate = sums[:, 2 * j * share : (2 * j + 1) * share]
-        up = sums[:, (2 * j + 1) * share : (2 * j + 2) * share]
-        acts.append((jax.nn.silu(gate) * up * scale[:, j : j + 1]).astype(bf16))
-    acts.append((jax.nn.silu(dense[:, :units]) * dense[:, units:]).astype(bf16))
-    part = jnp.dot(jnp.concatenate(acts, axis=1), w2, preferred_element_type=jnp.float32)
+    part = jnp.dot(acts, w2, preferred_element_type=jnp.float32)
     return reduce_sum(n, part.astype(bf16))
 
 

time: 159 us -> 145 us (0.912)
  matrix products: 18.2 us -> 6.83 us
    dot_general x3 -> x1, matrix products: 18.2 us -> 6.83 us  [by_kernels(): part = jnp.dot(acts, w2, preferred_element_type=jnp.float32)]
    unnamed x15 -> x9, local copies, waits for them, and re-layouts: 3.83 us -> 2.14 us
where the time goes in v5:
time: 145 us
  Pallas kernels  126 us (87%)
  matrix products  6.83 us (5%)
  local copies, waits for them, and re-layouts  4.85 us (3%)
  other arithmetic  4.68 us (3%)
  blocking collectives  2.58 us (2%)
    pallas_call x1, Pallas kernels, gather(): pl.pallas_call(functools.partial(gather_kernel, n), out_shape=(shape((n *...  91.1 us
    pallas_call x1, Pallas kernels, reduce_sum(): pl.pallas_call(functools.partial(reduce_kernel, n), out_shape=jax.ShapeDt...  34.7 us
    dot_general x1, matrix products, by_kernels(): part = jnp.dot(acts, w2, preferred_element_type=jnp.float32)  6.83 us

profile of v5, /device:TPU:0, one launch (start us, length us, event | category | flops | bytes accessed | tf_op | source)
XLA Modules:
  0.0 144.9 jit_solution(5021534740228027692)
XLA Ops:
  0.0 0.0 copy-start.2
  0.0 0.0 copy-start.1
  0.0 1.2 fusion.2
  1.2 2.6 %psum.7 = f32[128,1]{0,1:T(1,128)S(1)} all-reduce(f32[128,1]{0,1:T(1,128)S(1)} %bitcast.23), channel_id=1, replica_groups=mesh['groups'=2,'expert'=8,'hidden'=2] {'hidden'}, use_global_device_ids=true, to_apply=%region_1.0 | all-reduce | flops 128 | bytes 1024 | tf_op jit(solution)/shard_map/psum | solution.py:392
  3.8 0.7 dynamic_slice.3
  4.5 0.7 select_reduce_fusion
  5.2 1.1 fusion.3
  6.3 1.1 convert_bitcast_fusion
  7.4 0.1 pad_maximum_fusion.1.tok
  7.4 0.0 copy-done.1
  7.4 0.3 copy.20
  7.7 0.5 copy.21
  8.2 0.0 copy-done.2
  8.2 1.2 copy.22
  9.4 0.0 copy-start
  9.4 1.5 %copy.23 = bf16[256,8,192]{2,0,1:T(8,128)(2,1)S(1)} copy(bf16[256,8,192]{0,2,1:T(8,128)(2,1)} %bitcast.21) | data formatting | bytes 1572864 | tf_op jit(solution)/shard_map/reshape | solution.py:372
  10.9 0.6 pad_maximum_fusion.gu
  11.5 0.0 copy-done
  11.5 91.1 %shard_map.109 = (bf16[1024,960]{1,0:T(8,128)(2,1)S(1)}, bf16[960,2048]{1,0:T(8,128)(2,1)}) custom-call(bf16[2,128,1024]{2,1,0:T(8,128)(2,1)S(1)} %pad_maximum_fusion.1.tok, f32[8,8,128]{2,1,0:T(8,128)S(1)} %pad.4.gates, bf16[8,256,384]{2,1,0:T(8,128)(2,1)S(1)} %pad_maximum_fusion.gu, bf16[8,192,256]{2,1,0:T(8,128)(2,1)S(1)} %bitcast.17, ...), custom_call_target="tpu_custom_call" | custom-call | tf_op jit(solution)/shard_map/pallas_call | solution.py:238
  102.6 6.8 %convolution_convert_fusion.part = bf16[1024,2048]{1,0:T(8,128)(2,1)S(1)} fusion(bf16[1024,960]{1,0:T(8,128)(2,1)S(1)} %get-tuple-element.7, bf16[960,2048]{1,0:T(8,128)(2,1)} %get-tuple-element.8), kind=kOutput, calls=%fused_computation | convolution fusion | flops 4028628992 | bytes 10092544 | tf_op jit(solution)/shard_map/dot_general | solution.py:380
  109.5 34.7 %shard_map.110 = bf16[128,1024]{1,0:T(8,128)(2,1)S(1)} custom-call(bf16[1024,2048]{1,0:T(8,128)(2,1)S(1)} %convolution_convert_fusion.part), custom_call_target="tpu_custom_call" | custom-call | tf_op jit(solution)/shard_map/pallas_call | solution.py:340
  144.2 0.7 copy.25
  (2 shorter events, 0.0 us)
Async XLA Ops:
  0.0 8.2 %copy-start.2 = (bf16[256,1536]{1,0:T(8,128)(2,1)S(1)}, bf16[256,1536]{1,0:T(8,128)(2,1)}, u32[]{:S(2)}) copy-start(bf16[256,1536]{1,0:T(8,128)(2,1)} %param.20) | copy-start | bytes 2359300
  0.0 7.4 %copy-start.1 = (bf16[256,1536]{1,0:T(8,128)(2,1)S(1)}, bf16[256,1536]{1,0:T(8,128)(2,1)}, u32[]{:S(2)}) copy-start(bf16[256,1536]{1,0:T(8,128)(2,1)} %param.19) | copy-start | bytes 2359300
  9.4 2.1 %copy-start = (bf16[1536,256]{1,0:T(8,128)(2,1)S(1)}, bf16[1536,256]{1,0:T(8,128)(2,1)}, u32[]{:S(2)}) copy-start(bf16[1536,256]{1,0:T(8,128)(2,1)} %param.21) | copy-start | bytes 2359300

commit v6 on v5

--- a/solution.py
+++ b/solution.py
@@ -261,7 +261,7 @@
     )(tok, gates, gu, dn, eg, eu, ed)
 
 
-def reduce_kernel(n, part, out, core, sent, got, core_s, core_r, ring_s, ring_r):
+def reduce_kernel(n, acts, w2, out, part, core, sent, got, core_s, core_r, ring_s, ring_r):
     me, h = lax.axis_index("expert"), lax.axis_index("hidden")
     tokens, width = out.shape
     half = n // 2
@@ -276,8 +276,11 @@
         order += [d, -d]
     order.append(0)
     trades = {}
-    for k, d in enumerate(order):
+
+    def make(d):
+        k = order.index(d)
         rows = rows_of(ring_index(place + d, n), tokens)
+        part[rows] = jnp.dot(acts[rows], w2[...], preferred_element_type=jnp.float32).astype(jnp.bfloat16)
         trades[d] = remote(part.at[rows, theirs], core.at[rows], core_s.at[k], core_r.at[k], mate)
         trades[d].start()
 
@@ -298,6 +301,9 @@
             view(sent, step, way), view(got, step, way), ring_s.at[k], ring_r.at[k], right if way == 0 else left
         )
 
+    make(half)
+    make(half - 1)
+    make(1 - half)
     far = own(half).astype(jnp.bfloat16)
     hops = []
     for step in range(1, half + 1):
@@ -322,6 +328,11 @@
             copy = hop(step, way)
             copy.start()
             hops.append(copy)
+        d = half - 1 - step
+        if d >= 0:
+            make(d)
+        if d > 0:
+            make(-d)
     value = own(0)
     for way in range(2):
         hop(half, way).wait_recv()
@@ -333,16 +344,17 @@
         copy.wait_send()
 
 
-def reduce_sum(n, part):
-    tokens, width = part.shape[0] // n, part.shape[1] // 2
+def reduce_sum(n, acts, w2):
+    tokens, width = acts.shape[0] // n, w2.shape[1] // 2
     bf16 = jnp.bfloat16
     dma = lambda count: pltpu.SemaphoreType.DMA((count,))
     return pl.pallas_call(
         functools.partial(reduce_kernel, n),
         out_shape=jax.ShapeDtypeStruct((tokens, width), bf16),
-        in_specs=[pl.BlockSpec(memory_space=pltpu.VMEM)],
+        in_specs=[pl.BlockSpec(memory_space=pltpu.VMEM)] * 2,
         out_specs=pl.BlockSpec(memory_space=pltpu.VMEM),
         scratch_shapes=[
+            pltpu.VMEM((n * tokens, 2 * width), bf16),
             pltpu.VMEM((n * tokens, width), bf16),
             pltpu.VMEM((n, tokens, width), bf16),
             pltpu.VMEM((n, tokens, width), bf16),
@@ -351,7 +363,7 @@
         compiler_params=pltpu.CompilerParams(
             collective_id=1, has_side_effects=True, vmem_limit_bytes=40 * 2**20
         ),
-    )(part)
+    )(acts, w2)
 
 
 def kernel_fits(tokens, width, share, depth, units):
@@ -377,8 +389,7 @@
     acts, w2 = gather(
         n, jnp.stack([routed, normed]), packed, gu, dn, expert_gate, expert_up, expert_down
     )
-    part = jnp.dot(acts, w2, preferred_element_type=jnp.float32)
-    return reduce_sum(n, part.astype(bf16))
+    return reduce_sum(n, acts, w2)
 
 
 def own_gates(expert_ids, gate_values, experts_all):

time: 145 us -> 140 us (0.966)
  matrix products: 6.83 us -> 0 us
  local copies, waits for them, and re-layouts: 4.85 us -> 6.96 us
    dot_general x1 -> x0, matrix products: 6.83 us -> none  [by_kernels(): part = jnp.dot(acts, w2, preferred_element_type=jnp.float32)]
    unnamed x9 -> x11, local copies, waits for them, and re-layouts: 2.14 us -> 4.24 us
where the time goes in v6:
time: 140 us; the launch traced here: 139 us
  Pallas kernels  125 us (89%)
  local copies, waits for them, and re-layouts  6.96 us (5%)
  other arithmetic  4.68 us (3%)
  blocking collectives  2.58 us (2%)
    pallas_call x1, Pallas kernels, gather(): pl.pallas_call(functools.partial(gather_kernel, n), out_shape=(shape((n *...  91.1 us
    pallas_call x1, Pallas kernels, reduce_sum(): pl.pallas_call(functools.partial(reduce_kernel, n), out_shape=jax.ShapeDt...  34 us
    unnamed x11, local copies, waits for them, and re-layouts  4.24 us

profile of v6, /device:TPU:0, one launch (start us, length us, event | category | flops | bytes accessed | tf_op | source)
XLA Modules:
  0.0 139.5 jit_solution(9966679294233996899)
XLA Ops:
  0.0 0.0 copy-start.3
  0.0 0.0 copy-start.2
  0.0 1.2 fusion.2
  1.2 2.6 %psum.7 = f32[128,1]{0,1:T(1,128)S(1)} all-reduce(f32[128,1]{0,1:T(1,128)S(1)} %bitcast.21), channel_id=1, replica_groups=mesh['groups'=2,'expert'=8,'hidden'=2] {'hidden'}, use_global_device_ids=true, to_apply=%region_1.0 | all-reduce | flops 128 | bytes 1024 | tf_op jit(solution)/shard_map/psum | solution.py:403
  3.8 0.7 dynamic_slice.3
  4.5 0.7 select_reduce_fusion
  5.2 1.1 fusion.3
  6.3 1.1 convert_bitcast_fusion
  7.4 0.1 pad_maximum_fusion.1.tok
  7.4 0.0 copy-done.2
  7.4 0.3 copy.20
  7.7 0.5 copy.21
  8.2 0.0 copy-done.3
  8.2 1.2 copy.22
  9.4 0.0 copy-start.1
  9.4 1.5 %copy.23 = bf16[256,8,192]{2,0,1:T(8,128)(2,1)S(1)} copy(bf16[256,8,192]{0,2,1:T(8,128)(2,1)} %bitcast.19) | data formatting | bytes 1572864 | tf_op jit(solution)/shard_map/reshape | solution.py:384
  10.9 0.6 pad_maximum_fusion.gu
  11.5 0.0 copy-done.1
  11.5 91.1 %shard_map.109 = (bf16[1024,960]{1,0:T(8,128)(2,1)S(1)}, bf16[960,2048]{1,0:T(8,128)(2,1)}) custom-call(bf16[2,128,1024]{2,1,0:T(8,128)(2,1)S(1)} %pad_maximum_fusion.1.tok, f32[8,8,128]{2,1,0:T(8,128)S(1)} %pad.4.gates, bf16[8,256,384]{2,1,0:T(8,128)(2,1)S(1)} %pad_maximum_fusion.gu, bf16[8,192,256]{2,1,0:T(8,128)(2,1)S(1)} %bitcast.15, ...), custom_call_target="tpu_custom_call" | custom-call | tf_op jit(solution)/shard_map/pallas_call | solution.py:238
  102.6 0.0 copy-start
  102.6 2.1 %copy-done = bf16[960,2048]{1,0:T(8,128)(2,1)S(1)} copy-done((bf16[960,2048]{1,0:T(8,128)(2,1)S(1)}, bf16[960,2048]{1,0:T(8,128)(2,1)}, u32[]{:S(2)}) %copy-start) | copy-done | bytes 3932184
  104.8 34.0 %shard_map.110 = bf16[128,1024]{1,0:T(8,128)(2,1)S(1)} custom-call(bf16[1024,960]{1,0:T(8,128)(2,1)S(1)} %get-tuple-element.7.acts, bf16[960,2048]{1,0:T(8,128)(2,1)S(1)} %copy-done), custom_call_target="tpu_custom_call" | custom-call | tf_op jit(solution)/shard_map/pallas_call | solution.py:351
  138.8 0.7 copy.25
  (2 shorter events, 0.0 us)
Async XLA Ops:
  0.0 8.2 %copy-start.3 = (bf16[256,1536]{1,0:T(8,128)(2,1)S(1)}, bf16[256,1536]{1,0:T(8,128)(2,1)}, u32[]{:S(2)}) copy-start(bf16[256,1536]{1,0:T(8,128)(2,1)} %param.20) | copy-start | bytes 2359300
  0.0 7.4 %copy-start.2 = (bf16[256,1536]{1,0:T(8,128)(2,1)S(1)}, bf16[256,1536]{1,0:T(8,128)(2,1)}, u32[]{:S(2)}) copy-start(bf16[256,1536]{1,0:T(8,128)(2,1)} %param.19) | copy-start | bytes 2359300
  9.4 2.1 %copy-start.1 = (bf16[1536,256]{1,0:T(8,128)(2,1)S(1)}, bf16[1536,256]{1,0:T(8,128)(2,1)}, u32[]{:S(2)}) copy-start(bf16[1536,256]{1,0:T(8,128)(2,1)} %param.21) | copy-start | bytes 2359300
  102.6 2.1 %copy-start = (bf16[960,2048]{1,0:T(8,128)(2,1)S(1)}, bf16[960,2048]{1,0:T(8,128)(2,1)}, u32[]{:S(2)}) copy-start(bf16[960,2048]{1,0:T(8,128)(2,1)} %get-tuple-element.8.w2) | copy-start | bytes 11796484
